TPU v7x, 32 devices: a whole 2x2x4 slice. The times are simulated.
32 devices in a mesh: row: 4 (over y, x), col: 8 (over z, core).
Axes of the slice: x: 2, y: 2, z: 4, core: 2. Of those that a mesh axis runs over, the one named last changes fastest.
Arguments:
- tokens: bfloat16 [16384, 1024], P(('row', 'col')), may hold values from -6 to 6
- gain_attn: bfloat16 [1024], P(('row', 'col')), may hold values from 0.099609375 to 1.8984375
- w_query: bfloat16 [1024, 1024], P(('row', 'col')), may hold values from -0.1875 to 0.1875
- w_keyval: bfloat16 [1024, 256], P(('row', 'col')), may hold values from -0.1875 to 0.1875
- w_out: bfloat16 [1024, 1024], P(('row', 'col')), may hold values from -3 to 3
- gain_mlp: bfloat16 [1024], P(('row', 'col')), may hold values from 0.099609375 to 1.8984375
- w_gate: bfloat16 [1024, 3072], P('row', 'col'), may hold values from -0.1875 to 0.1875
- w_up: bfloat16 [1024, 3072], P('row', 'col'), may hold values from -0.1875 to 0.1875
- w_down: bfloat16 [3072, 1024], P('col', 'row'), may hold values from -0.109375 to 0.109375
- segment: int32 [16384], P(('row', 'col')), may hold values from 0 to 15, as said below
- cotangent: bfloat16 [16384, 1024], P(('row', 'col')), may hold values from -6 to 6
Outputs:
- output: bfloat16 [16384, 1024], P(('row', 'col'))
- grad_tokens: float32 [16384, 1024], P(('row', 'col'))
- grad_gain_attn: float32 [1024], P(('row', 'col'))
- grad_query: float32 [1024, 1024], P(('row', 'col'))
- grad_keyval: float32 [1024, 256], P(('row', 'col'))
- grad_out: float32 [1024, 1024], P(('row', 'col'))
- grad_gain_mlp: float32 [1024], P(('row', 'col'))
- grad_gate: float32 [1024, 3072], P('row', 'col')
- grad_up: float32 [1024, 3072], P('row', 'col')
- grad_down: float32 [3072, 1024], P('col', 'row')
Inputs may be any that keep to these rules, and one draw needn't show every extreme that they name: `segment`: never falling; each pack of 2048 tokens holds two documents, numbered 2p and 2p + 1 for pack p; the first one is 512 to 1536 tokens long.
All inputs are finite; a program needn't handle non-finite values.
Results may differ from a plain program's by a relative error of at most 0.014.
Values may be sent and summed in bfloat16 or wider, within the bound.
A program may use at most 256 MiB of HBM per device.

v0:
```python
import functools
import math

import jax
import jax.numpy as jnp
from jax import lax
from jax.experimental import pallas as pl
from jax.experimental.pallas import tpu as pltpu
from jax.sharding import PartitionSpec as P

H = 8
DH = 128
WINDOW = 1024
PACK = 2048

EPS = 1e-06
NEGATIVE = -1e30
MESH = pl.DeviceIdType.MESH
BF = jnp.bfloat16
F32 = jnp.float32


def product(left, right):
    return jnp.dot(left, right, preferred_element_type=jnp.float32)


def against(left, right):
    return lax.dot_general(
        left, right, (((1,), (1,)), ((), ())), preferred_element_type=jnp.float32
    )


class Place:
    def __init__(self, shape):
        rows, cols = shape
        self.X = math.isqrt(rows)
        while rows % self.X:
            self.X -= 1
        self.Y = rows // self.X
        self.Z = cols // 2
        self.R = rows
        self.row, self.col = lax.axis_index("row"), lax.axis_index("col")
        self.y, self.x = self.row // self.X, self.row % self.X
        self.z, self.core = self.col // 2, self.col % 2
        self.xs, self.ys, self.zs = range(1, self.X), range(1, self.Y), range(1, self.Z)

    def row_at(self, dy=0, dx=0):
        return lax.rem(self.y + dy + self.Y, self.Y) * self.X + lax.rem(
            self.x + dx + self.X, self.X
        )

    def z_at(self, dz):
        return lax.rem(self.z + dz + self.Z, self.Z)

    def device(self, dy=0, dx=0, dz=0, other=False):
        core = 1 - self.core if other else self.core
        return (self.row_at(dy, dx), self.z_at(dz) * 2 + core)


def remote(src, dst, send, recv, device):
    return pltpu.make_async_remote_copy(
        src_ref=src, dst_ref=dst, send_sem=send, recv_sem=recv, device_id=device,
        device_id_type=MESH,
    )


class Sems:
    def __init__(self, send, recv):
        self.send, self.recv, self.count = send, recv, 0

    def take(self):
        self.count += 1
        return self.send.at[self.count - 1], self.recv.at[self.count - 1]


def gather_count(X, Y, Z):
    return (Z - 1) + Z * ((X - 1) + (Y - 1) + 2 * (X - 1) * (Y - 1))


class Gather:
    def __init__(self, at, here, sems, own):
        self.at, self.p, self.own = at, here, own
        self.sent = []
        p = here
        self.zsem = {k: sems.take() for k in p.zs}
        self.xsem = {(s, d): sems.take() for s in range(p.Z) for d in p.xs}
        self.ysem = {(s, d): sems.take() for s in range(p.Z) for d in p.ys}
        self.dsem = {
            (s, h, dx, dy): sems.take()
            for s in range(p.Z) for h in (0, 1) for dx in p.xs for dy in p.ys
        }

    def push(self, src, dst, sem, device):
        copy = remote(src, dst, sem[0], sem[1], device)
        copy.start()
        self.sent.append(copy)

    def arrive(self, place, sem):
        remote(place, place, sem[0], sem[1], self.p.device(other=True)).wait_recv()

    def spread_z(self):
        p = self.p
        for k in p.zs:
            self.push(self.own, self.at(p.z, p.row, None), self.zsem[k], p.device(dz=-k))

    def spread_xy(self, s):
        p = self.p
        zc = p.z_at(s)
        place = self.at(zc, p.row, None)
        src = self.own
        if s:
            self.arrive(place, self.zsem[s])
            src = place
        for d in p.xs:
            self.push(src, place, self.xsem[s, d], p.device(dx=d))
        for d in p.ys:
            self.push(src, place, self.ysem[s, d], p.device(dy=d))

    def spread_diagonal(self, s):
        p = self.p
        zc = p.z_at(s)
        for d in p.xs:
            r = p.row_at(dx=-d)
            self.arrive(self.at(zc, r, None), self.xsem[s, d])
            half = self.at(zc, r, 0)
            for e in p.ys:
                self.push(half, half, self.dsem[s, 0, d, e], p.device(dy=e))
        for e in p.ys:
            r = p.row_at(dy=-e)
            self.arrive(self.at(zc, r, None), self.ysem[s, e])
            half = self.at(zc, r, 1)
            for d in p.xs:
                self.push(half, half, self.dsem[s, 1, d, e], p.device(dx=d))

    def close(self, s):
        p = self.p
        zc = p.z_at(s)
        for d in p.xs:
            for e in p.ys:
                r = p.row_at(dy=-e, dx=-d)
                for h in (0, 1):
                    self.arrive(self.at(zc, r, h), self.dsem[s, h, d, e])

    def finish(self):
        for copy in self.sent:
            copy.wait_send()


def scatter_count(X, Y, Z):
    return (Z - 1) + Z * (2 * (X - 1) * (Y - 1) + 2 * (X - 1) + 2 * (Y - 1))


class Scatter:
    def __init__(self, part, cut, here, sems, termx, termy, own, diag, fromx, fromy, fromz):
        self.part, self.cut, self.p = part, cut, here
        self.termx, self.termy, self.own = termx, termy, own
        self.diag, self.fromx, self.fromy, self.fromz = diag, fromx, fromy, fromz
        self.sent = []
        p = here
        self.zsem = {k: sems.take() for k in p.zs}
        self.xsem = {(s, h, d): sems.take() for s in range(p.Z) for h in (0, 1) for d in p.xs}
        self.ysem = {(s, h, d): sems.take() for s in range(p.Z) for h in (0, 1) for d in p.ys}
        self.dsem = {
            (s, h, dx, dy): sems.take()
            for s in range(p.Z) for h in (0, 1) for dx in p.xs for dy in p.ys
        }

    def push(self, src, dst, sem, device):
        copy = remote(src, dst, sem[0], sem[1], device)
        copy.start()
        self.sent.append(copy)

    def arrive(self, place, sem):
        remote(place, place, sem[0], sem[1], self.p.device(other=True)).wait_recv()

    def spot(self, d, e):
        return (d - 1) * (self.p.Y - 1) + e - 1

    def first(self, s):
        p, cut = self.p, self.cut
        zc = p.z_at(s)
        for d in p.xs:
            for e in p.ys:
                far = self.part(zc, p.row_at(dy=e, dx=d))
                n = self.spot(d, e)
                self.push(cut(far, 0), self.diag.at[s, 0, n], self.dsem[s, 0, d, e], p.device(dx=d))
                self.push(cut(far, 1), self.diag.at[s, 1, n], self.dsem[s, 1, d, e], p.device(dy=e))
        for d in p.xs:
            near = self.part(zc, p.row_at(dx=d))
            self.push(cut(near, 0), cut(self.fromx.at[s, d - 1], 0), self.xsem[s, 0, d], p.device(dx=d))
        for e in p.ys:
            near = self.part(zc, p.row_at(dy=e))
            self.push(cut(near, 1), cut(self.fromy.at[s, e - 1], 1), self.ysem[s, 1, e], p.device(dy=e))

    def second(self, s):
        p, cut = self.p, self.cut
        for e in p.ys:
            term = self.termy(s, e)
            total = term[...].astype(F32)
            for d in p.xs:
                place = self.diag.at[s, 0, self.spot(d, e)]
                self.arrive(place, self.dsem[s, 0, d, e])
                total = total + place[...].astype(F32)
            term[...] = total.astype(BF)
            self.push(term, cut(self.fromy.at[s, e - 1], 0), self.ysem[s, 0, e], p.device(dy=e))
        for d in p.xs:
            term = self.termx(s, d)
            total = term[...].astype(F32)
            for e in p.ys:
                place = self.diag.at[s, 1, self.spot(d, e)]
                self.arrive(place, self.dsem[s, 1, d, e])
                total = total + place[...].astype(F32)
            term[...] = total.astype(BF)
            self.push(term, cut(self.fromx.at[s, d - 1], 1), self.xsem[s, 1, d], p.device(dx=d))

    def third(self, s, out=None):
        p, cut = self.p, self.cut
        own = self.own(s)
        total = own[...].astype(F32)
        for d in p.xs:
            for h in (0, 1):
                self.arrive(cut(self.fromx.at[s, d - 1], h), self.xsem[s, h, d])
            total = total + self.fromx[s, d - 1].astype(F32)
        for e in p.ys:
            for h in (0, 1):
                self.arrive(cut(self.fromy.at[s, e - 1], h), self.ysem[s, h, e])
            total = total + self.fromy[s, e - 1].astype(F32)
        if s:
            own[...] = total.astype(BF)
            self.push(own, self.fromz.at[s - 1], self.zsem[s], p.device(dz=s))
            return
        for k in p.zs:
            self.arrive(self.fromz.at[k - 1], self.zsem[k])
            total = total + self.fromz[k - 1].astype(F32)
        out[...] = total

    def finish(self):
        for copy in self.sent:
            copy.wait_send()


def scatter_scratch(X, Y, Z, block):
    half = (block[0] // 2, block[1])
    return [
        pltpu.VMEM((Z, 2, (X - 1) * (Y - 1)) + half, BF),
        pltpu.VMEM((Z, X - 1) + block, BF),
        pltpu.VMEM((Z, Y - 1) + block, BF),
        pltpu.VMEM((Z - 1,) + block, BF),
    ]


def sides(shape):
    x = math.isqrt(shape[0])
    while shape[0] % x:
        x -= 1
    return x, shape[0] // x, shape[1] // 2


VM = pl.BlockSpec(memory_space=pltpu.VMEM)
ANY = pl.BlockSpec(memory_space=pl.ANY)
DMA = pltpu.SemaphoreType.DMA
LOG2E = math.log2(math.e)
BLOCK = 256


def loop(count, body):
    def step(t, carry):
        body(t)
        return carry

    lax.fori_loop(0, count, step, 0)


def at(t, size):
    return pl.ds(pl.multiple_of(t * size, size), size)


def rms_scale(value):
    return lax.rsqrt(jnp.mean(value * value, axis=-1, keepdims=True) + EPS)


def gelu_parts(gate):
    square = gate * gate
    t = jnp.tanh(gate * (0.7978845608 + (0.7978845608 * 0.044715) * square))
    half = 0.5 + 0.5 * t
    slope = half + (0.5 * gate) * (1.0 - t * t) * (
        0.7978845608 + (3 * 0.7978845608 * 0.044715) * square
    )
    return gate * half, slope


def forward_kernel(shape, with_slab, sizes, *refs):
    D, T, E, W, hz = sizes
    (tokens, cot, marks, slab, ffn,
     output, grad_in, middle, slabs_out, query_out, window_out, bias_out, att_out, lse_out, grads_out,
     slabs, ffns, query, window, values_t, marks_all, bias, att, lse, gains, mlp, mlp_t, cots, cots_t,
     grad_sum, out_sum, hidden, grad_act, stage, out_send,
     asend, arecv, fsend, frecv, csend, crecv, ksend, krecv, xsend, xrecv, lsem, gsem) = refs
    p = Place(shape)
    pack = PACK // T
    spot = lax.rem(p.col, pack)
    QK = E + 2 * DH
    B = T // BLOCK
    span = WINDOW + BLOCK
    loads = []

    def local(src, dst, n):
        copy = pltpu.make_async_copy(src, dst, lsem.at[n])
        copy.start()
        return copy

    barrier = pltpu.get_barrier_semaphore()
    across = (p.row, lax.rem(p.z + 1, 2) + p.z // 2 * 2)
    across = (across[0], across[1] * 2 + 1 - p.core)
    mates = [p.device(dx=d) for d in p.xs] + [p.device(dy=d) for d in p.ys]
    mates += [p.device(dz=d) for d in p.zs] + [p.device(other=True), across]
    for mate in mates:
        pl.semaphore_signal(barrier, inc=1, device_id=mate, device_id_type=MESH)
    load_cot = local(cot, cots.at[pl.ds(0, T)], 0)
    if not with_slab:
        load_slab = local(slab, slabs, 1)
    pl.semaphore_wait(barrier, len(mates))
    mate = p.device(other=True)

    br = ffn.shape[0]

    def ffn_at(zc, r, half):
        if half is None:
            return ffns.at[zc, at(r, br)]
        return ffns.at[zc, pl.ds(pl.multiple_of(r * br + half * (br // 2), br // 2), br // 2)]

    far = Gather(ffn_at, p, Sems(fsend, frecv), ffn)

    if with_slab:
        ar = slab.shape[0]

        def slab_row(r, zc, core):
            return ((r * p.Z + zc) * 2 + core) * ar

        def slab_at(zc, r, half):
            if half is None:
                return slabs.at[pl.ds(pl.multiple_of(slab_row(r, zc, p.core), ar), ar)]
            return slabs.at[
                pl.ds(pl.multiple_of(slab_row(r, zc, p.core) + half * (ar // 2), ar // 2), ar // 2)
            ]

        near = Gather(slab_at, p, Sems(asend, arecv), slab)
        near.spread_z()
        near.spread_xy(0)

    load_cot.wait()
    cot_copy = remote(cots.at[pl.ds(0, T)], cots.at[pl.ds(T, T)], xsend.at[0], xrecv.at[0], mate)
    cot_copy.start()
    marks_all[:, pl.ds(2 * T, T)] = marks[...]

    @pl.when(spot == 0)
    def _():
        window[pl.ds(0, 2 * T), :] = jnp.zeros((2 * T, 2 * DH), BF)
        marks_all[:, pl.ds(0, 2 * T)] = jnp.full((8, 2 * T), -1.0, F32)

    @pl.when(spot == 1)
    def _():
        window[pl.ds(0, T), :] = jnp.zeros((T, 2 * DH), BF)
        marks_all[:, pl.ds(0, T)] = jnp.full((8, T), -1.0, F32)

    def behind(src, place, n, op):
        for d in (1, 2):
            to = (p.row, lax.rem(p.col + d, 2 * p.Z))
            copy = remote(src, place(2 - d), ksend.at[n + d], krecv.at[n + d], to)
            if op == "start":
                pl.when(spot + d < pack)(copy.start)
            elif op == "arrive":
                pl.when(spot - d >= 0)(copy.wait_recv)
            else:
                pl.when(spot + d < pack)(copy.wait_send)

    mark_place = lambda k: marks_all.at[:, pl.ds(k * T, T)]
    mark_own = mark_place(2)
    behind(mark_own, mark_place, 0, "start")
    if with_slab:
        slabs[pl.ds(pl.multiple_of(slab_row(p.row, p.z, p.core), ar), ar)] = slab[...]
    ffns[p.z, at(p.row, br)] = ffn[...]

    def turn_cot(t):
        cots_t[:, at(t, BLOCK)] = cots[at(t, BLOCK)].T

    loop(B, turn_cot)
    if with_slab:
        for s in range(p.Z):
            if s + 1 < p.Z:
                near.spread_xy(s + 1)
            near.spread_diagonal(s)
        far.spread_z()
        far.spread_xy(0)
        passed = []
        n = 0
        for s in range(p.Z):
            near.close(s)
            zc = p.z_at(s)
            for dy in range(p.Y):
                for dx in range(p.X):
                    r = p.row_at(dy, dx)
                    place = slab_at(zc, r, None)
                    copy = remote(place, place, csend.at[n], crecv.at[n], mate)
                    copy.start()
                    theirs = slabs.at[pl.ds(pl.multiple_of(slab_row(r, zc, 1 - p.core), ar), ar)]
                    passed.append((copy, remote(theirs, theirs, csend.at[n], crecv.at[n], mate)))
                    n += 1
        cot_copy.wait()
        loop(B, lambda t: turn_cot(t + B))
        for copy, arrival in passed:
            copy.wait_send()
            arrival.wait_recv()
    else:
        far.spread_z()
        far.spread_xy(0)
        cot_copy.wait()
        loop(B, lambda t: turn_cot(t + B))
        load_slab.wait()
    save_slabs = local(slabs, slabs_out, 1)
    gains[...] = slabs[:, QK + E :].astype(F32).T[0:8]

    def first_norm(t):
        rows = at(t, 64)
        value = tokens[rows].astype(F32)
        mlp[rows] = (value * rms_scale(value) * gains[0:1]).astype(BF)

    loop(T // 64, first_norm)
    window[pl.ds(2 * T, T)] = product(mlp[pl.ds(0, T)], slabs[:, E : E + 2 * DH]).astype(BF)
    key_place = lambda k: window.at[pl.ds(k * T, T)]
    behind(key_place(2), key_place, 3, "start")

    def project(t):
        query[at(t, BLOCK)] = product(mlp[at(t, BLOCK)], slabs[:, 0:E]).astype(BF)

    loop(B, project)
    if p.Z > 1:
        far.spread_xy(1)
    save_query = local(query, query_out, 2)
    behind(mark_own, mark_place, 0, "arrive")
    column = jnp.broadcast_to(marks_all[0:1], (128, 3 * T)).T
    for i in range(B):
        keys_at = jnp.concatenate([column[i * BLOCK : i * BLOCK + span]] * (BLOCK // 128), axis=1)
        own = marks_all[0:1, 2 * T + i * BLOCK : 2 * T + (i + 1) * BLOCK]
        gap = (
            WINDOW
            + lax.broadcasted_iota(jnp.int32, (span, BLOCK), 1)
            - lax.broadcasted_iota(jnp.int32, (span, BLOCK), 0)
        )
        allowed = (keys_at == own) & (gap >= 0) & (gap < WINDOW)
        bias[i] = jnp.where(allowed, 0.0, NEGATIVE)
    save_bias = local(bias, bias_out, 3)
    behind(key_place(2), key_place, 3, "arrive")
    save_window = local(window, window_out, 4)
    values_t[...] = window[:, DH:].T
    factor = LOG2E / math.sqrt(DH)

    def head(i, h):
        lanes = at(h, DH)
        keys = window[pl.ds(i * BLOCK, span), 0:DH]
        scores = against(keys, query[pl.ds(i * BLOCK, BLOCK), lanes]) * factor + bias[i]
        top = jnp.max(scores, axis=0, keepdims=True)
        expo = jnp.exp2(scores - top)
        total = jnp.sum(expo, axis=0, keepdims=True)
        mixed = product(values_t[:, pl.ds(i * BLOCK, span)], expo.astype(BF))
        att[lanes, pl.ds(i * BLOCK, BLOCK)] = (mixed / total).astype(BF)
        lse[h * B + i] = jnp.broadcast_to(top + jnp.log2(total), (8, BLOCK))

    far.spread_diagonal(0)
    for i in range(B):
        loop(H // 2, lambda h: head(i, h))
        if i == 0 and p.Z > 2:
            far.spread_xy(2)
        loop(H // 2, lambda h: head(i, h + H // 2))
        if i == 0 and p.Z > 1:
            far.spread_diagonal(1)
    save_att = local(att, att_out, 5)
    save_lse = local(lse, lse_out, 6)

    def out_project(t):
        cols = at(t, BLOCK)
        middle[cols] = product(att[:, cols].T, slabs[:, QK : QK + E]) + tokens[cols].astype(F32)

    loop(B, out_project)

    def second_norm(t):
        rows = at(t, 64)
        value = middle[rows]
        mlp[rows] = (value * rms_scale(value) * gains[1:2]).astype(BF)

    loop(T // 64, second_norm)
    mlp_copy = remote(mlp.at[pl.ds(0, T)], mlp.at[pl.ds(T, T)], xsend.at[1], xrecv.at[1], mate)
    mlp_copy.start()

    def turn_mlp(t):
        mlp_t[:, at(t, BLOCK)] = mlp[at(t, BLOCK)].T

    loop(B, turn_mlp)
    if p.Z > 3:
        far.spread_xy(3)
    mlp_copy.wait()
    loop(B, lambda t: turn_mlp(t + B))
    for s in range(4, p.Z):
        far.spread_xy(s)

    saves = []
    for s in range(p.Z):
        zc = p.z_at(s)
        if s + 2 < p.Z:
            far.spread_diagonal(s + 2)
        far.close(s)
        slot = s % 2

        def tile(t):
            rows = at(t, BLOCK)
            gate_up = product(mlp[rows], ffns[zc, :, 0 : 2 * hz])
            grad_hidden = product(cots[rows], ffns[zc, :, 2 * hz :])
            up = gate_up[:, hz:]
            act, slope = gelu_parts(gate_up[:, :hz])
            hid = (act * up).astype(BF)
            hidden[rows] = hid
            grad_gate = (grad_hidden * up * slope).astype(BF)
            grad_up = (grad_hidden * act).astype(BF)
            grad_act[rows, 0:hz] = grad_gate
            grad_act[rows, hz : 2 * hz] = grad_up
            outs = against(hid, ffns[zc, :, 2 * hz :])
            grads = against(grad_act[rows], ffns[zc, :, 0 : 2 * hz])
            if s == 0:
                out_sum[rows] = outs
                grad_sum[rows] = grads
            else:
                out_sum[rows] += outs
                grad_sum[rows] += grads

        loop(2 * B, tile)
        if s > 1:
            saves[s - 2].wait()

        def weight_tile(t):
            rows = at(t, BLOCK)
            stage[slot, rows, 0 : 2 * hz] = product(mlp_t[rows], grad_act[...]).astype(BF)
            stage[slot, rows, 2 * hz :] = product(cots_t[rows], hidden[...]).astype(BF)

        loop(D // BLOCK, weight_tile)
        save = pltpu.make_async_copy(stage.at[slot], grads_out.at[zc], gsem.at[s])
        save.start()
        saves.append(save)

    grad_copy = remote(grad_sum.at[pl.ds(T, T)], grad_in, xsend.at[2], xrecv.at[2], mate)
    grad_copy.start()

    def narrow(t):
        out_send[at(t, 64)] = out_sum[pl.ds(pl.multiple_of(T + t * 64, 64), 64)].astype(BF)

    loop(T // 64, narrow)
    out_copy = remote(out_send, output, xsend.at[3], xrecv.at[3], mate)
    out_copy.start()
    for save in saves[max(0, p.Z - 2) :]:
        save.wait()
    for save in (save_slabs, save_query, save_bias, save_window, save_att, save_lse):
        save.wait()
    behind(mark_own, mark_place, 0, "sent")
    behind(key_place(2), key_place, 3, "sent")
    if with_slab:
        near.finish()
    far.finish()
    grad_copy.wait()

    def join(t):
        rows = at(t, 64)
        grad_in[rows] = grad_in[rows] + grad_sum[rows]

    loop(T // 64, join)
    out_copy.wait()

    def join_out(t):
        rows = at(t, 64)
        output[rows] = (middle[rows] + out_sum[rows] + output[rows].astype(F32)).astype(BF)

    loop(T // 64, join_out)


def forward(shape, with_slab, tokens, cot, marks, slab, ffn):
    X, Y, Z = sides(shape)
    T, D = tokens.shape
    E, hz = H * DH, ffn.shape[1] // 3
    W = slab.shape[1]
    B = T // BLOCK
    span = WINDOW + BLOCK
    n = gather_count(X, Y, Z)
    S = jax.ShapeDtypeStruct
    outs = [
        S((T, D), BF), S((T, D), F32), S((T, D), F32),
        S((D, W), BF), S((T, E), BF), S((3 * T, 2 * DH), BF), S((B, span, BLOCK), F32),
        S((E, T), BF), S((H * B, 8, BLOCK), F32), S((Z, D, 3 * hz), BF),
    ]
    V = pltpu.VMEM
    scratch = [
        V((D, W), BF), V((Z, D, 3 * hz), BF), V((T, E), BF), V((3 * T, 2 * DH), BF),
        V((DH, 3 * T), BF), V((8, 3 * T), F32), V((B, span, BLOCK), F32), V((E, T), BF),
        V((H * B, 8, BLOCK), F32), V((8, D), F32), V((2 * T, D), BF), V((D, 2 * T), BF),
        V((2 * T, D), BF), V((D, 2 * T), BF), V((2 * T, D), F32), V((2 * T, D), F32),
        V((2 * T, hz), BF), V((2 * T, 2 * hz), BF), V((2, D, 3 * hz), BF), V((T, D), BF),
        DMA((n,)), DMA((n,)), DMA((n,)), DMA((n,)),
        DMA((shape[0] * Z,)), DMA((shape[0] * Z,)), DMA((6,)), DMA((6,)), DMA((4,)), DMA((4,)),
        DMA((7,)), DMA((Z,)),
    ]
    return pl.pallas_call(
        functools.partial(forward_kernel, shape, with_slab, (D, T, E, W, hz)),
        out_shape=outs,
        in_specs=[VM, ANY, VM, VM if with_slab else ANY, VM],
        out_specs=[VM] * 3 + [ANY] * 7,
        scratch_shapes=scratch,
        compiler_params=pltpu.CompilerParams(
            collective_id=0, has_side_effects=True, vmem_limit_bytes=62 << 20
        ),
        name="forward",
    )(tokens, cot, marks, slab, ffn)


def backward_kernel(shape, with_slab, sizes, *refs):
    D, T, E, W, hz = sizes
    QK = E + 2 * DH
    B = T // BLOCK
    span = WINDOW + BLOCK
    (tokens_in, cot_in, middle_in, grad_in_in, slabs_in, query_in, window_in, bias_in, att_in, lse_in, grads,
     grad_tokens, ffn_out, out_slab, act_slab) = refs[:15]
    (tokens, cot, middle, grad_in, slabs, query, window, bias, att, lse,
     gains, keys_t, branch, att_grad, query_grad_t, query_grad, kv_sum, kv_send, kv_recv, kv_grad, attn_in_t,
     out_grads, act_grads, gain_rows, termx, termy, own) = refs[15:42]
    fwork = refs[42:46]
    rest = refs[46:]
    if with_slab:
        out_cross, act_cross = rest[:2]
        owork, awork = rest[2:6], rest[6:10]
        (fsend, frecv, ksend, krecv, lsem, psem, tsem, osend, orecv, asend, arecv, xsend, xrecv) = rest[10:]
    else:
        fsend, frecv, ksend, krecv, lsem, psem, tsem = rest
    p = Place(shape)
    pack = PACK // T
    spot = lax.rem(p.col, pack)
    mate = p.device(other=True)

    barrier = pltpu.get_barrier_semaphore()
    across = (p.row, (lax.rem(p.z + 1, 2) + p.z // 2 * 2) * 2 + 1 - p.core)
    mates = [p.device(dx=d) for d in p.xs] + [p.device(dy=d) for d in p.ys]
    mates += [p.device(dz=d) for d in p.zs] + [mate, across]
    for other in mates:
        pl.semaphore_signal(barrier, inc=1, device_id=other, device_id_type=MESH)

    br = D // p.R

    def part(zc, r):
        return grads.at[zc, at(r, br)]

    def cut(ref, h):
        rows = ref.shape[0] // 2
        return ref.at[pl.ds(h * rows, rows)]

    order = list(range(1, p.Z)) + [0]
    terms = {}
    for s in order:
        zc = p.z_at(s)
        copies = []
        n = s * (p.X + p.Y - 1)
        for d in p.xs:
            copies.append((cut(part(zc, p.row_at(dx=d)), 1), termx.at[s, d - 1]))
        for e in p.ys:
            copies.append((cut(part(zc, p.row_at(dy=e)), 0), termy.at[s, e - 1]))
        copies.append((part(zc, p.row), own.at[s]))
        terms[s] = [
            pltpu.make_async_copy(a, b, tsem.at[n + i]) for i, (a, b) in enumerate(copies)
        ]
    pairs = [
        (middle_in, middle), (grad_in_in, grad_in), (cot_in, cot), (slabs_in, slabs), (att_in, att),
        (tokens_in, tokens), (window_in, window), (query_in, query), (bias_in, bias), (lse_in, lse),
    ]
    loads = [pltpu.make_async_copy(a, b, lsem.at[n]) for n, (a, b) in enumerate(pairs)]
    for load in loads:
        load.start()
    for s in order:
        for copy in terms[s]:
            copy.start()
    pl.semaphore_wait(barrier, len(mates))
    far = Scatter(
        part, cut, p, Sems(fsend, frecv),
        lambda s, d: termx.at[s, d - 1], lambda s, e: termy.at[s, e - 1], lambda s: own.at[s], *fwork
    )
    ticks = []
    for j in range(p.Z + 1):
        tick = []
        if j >= 1:
            tick.append((far.third, order[j - 1]))
        if j < p.Z:
            tick.append((far.second, order[j]))
        if j + 2 < p.Z:
            tick.append((far.first, order[j + 2]))
        ticks.append(tick)

    def advance():
        if ticks:
            for step, s in ticks.pop(0):
                if step == far.second:
                    for copy in terms[s]:
                        copy.wait()
                if step == far.third:
                    step(s, ffn_out)
                else:
                    step(s)

    for s in order[:2]:
        far.first(s)

    for load in loads[:4]:
        load.wait()
    gains[...] = slabs[:, QK + E :].astype(F32).T[0:8]
    gain_rows[...] = jnp.zeros_like(gain_rows)

    def fold_rows(value):
        return jnp.sum(value.reshape(value.shape[0] // 8, 8, D), axis=0)

    def second_norm(t, total):
        rows = at(t, 64)
        value, grad = middle[rows], grad_in[rows]
        scale = rms_scale(value)
        total = total + fold_rows(grad * (value * scale))
        n = grad * gains[1:2]
        out = cot[rows].astype(F32) + scale * n - value * (
            scale * scale * scale * jnp.mean(n * value, axis=-1, keepdims=True)
        )
        grad_in[rows] = out
        branch[rows] = out.astype(BF)
        return total

    total = lax.fori_loop(0, T // 64, second_norm, jnp.zeros((8, D), F32))
    gain_rows[1:2] = jnp.sum(total, axis=0, keepdims=True)

    def attended_grad(t):
        att_grad[at(t, BLOCK)] = against(
            slabs[at(t, BLOCK), QK : QK + E], branch[...]
        ).astype(BF)

    loop(E // BLOCK, attended_grad)
    loads[4].wait()
    ar = D // (p.R * p.Z * 2)
    blocks = BLOCK // (2 * ar)

    def put(ref, t, lanes, value):
        ref[pl.ds(t * blocks, blocks), :, :, lanes] = value.astype(BF).reshape(
            blocks, 2, ar, value.shape[1]
        )

    if not with_slab:
        def put(ref, t, lanes, value):
            ref[at(t, BLOCK), lanes] = value.astype(BF)

    def out_weight_grad(t):
        put(out_grads, t, slice(0, E), product(att[at(t, BLOCK)], branch[...]))

    loop(E // BLOCK, out_weight_grad)

    def crossing(ref, place, n):
        return remote(ref.at[:, 1 - p.core], place, xsend.at[n], xrecv.at[n], mate)

    def fold(ref, place):
        def step(n):
            ref[n, p.core] = (ref[n, p.core].astype(F32) + place[n].astype(F32)).astype(BF)

        loop(p.R * p.Z, step)

    def plane_scatter(ref, sems, work):
        def block(zc, r):
            return ref.at[r * p.Z + zc, p.core]

        return Scatter(
            block, cut, p, sems,
            lambda s, d: cut(block(p.z_at(s), p.row_at(dx=d)), 1),
            lambda s, e: cut(block(p.z_at(s), p.row_at(dy=e)), 0),
            lambda s: block(p.z_at(s), p.row), *work
        )

    if with_slab:
        out_copy = crossing(out_grads, out_cross, 0)
        out_copy.start()
        near_out = plane_scatter(out_grads, Sems(osend, orecv), owork)
        near_act = plane_scatter(act_grads, Sems(asend, arecv), awork)

    for load in loads[5:]:
        load.wait()

    def first_norm(t):
        cols = at(t, 128)
        value = tokens[cols].astype(F32)
        attn_in_t[:, cols] = (value * rms_scale(value) * gains[0:1]).astype(BF).T

    loop(T // 128, first_norm)
    keys_t[...] = window[:, 0:DH].T
    kv_sum[...] = jnp.zeros_like(kv_sum)
    advance()

    factor = LOG2E / math.sqrt(DH)
    scale = 1.0 / math.sqrt(DH)

    def head(i, h):
        lanes = at(h, DH)
        here = pl.ds(i * BLOCK, BLOCK)
        seen = pl.ds(i * BLOCK, span)
        part_query = query[here, lanes]
        part_grad = att_grad[lanes, here]
        scores = against(window[seen, 0:DH], part_query) * factor + bias[i]
        probs = jnp.exp2(scores - lse[h * B + i][0:1])
        grad_probs = product(window[seen, DH:], part_grad)
        centre = jnp.sum(
            att[lanes, here].astype(F32) * part_grad.astype(F32), axis=0, keepdims=True
        )
        grad_scores = (probs * (grad_probs - centre)).astype(BF)
        kv_sum[seen, DH:] += against(probs.astype(BF), part_grad)
        kv_sum[seen, 0:DH] += product(grad_scores, part_query)
        query_grad_t[lanes, here] = (product(keys_t[:, seen], grad_scores) * scale).astype(BF)

    pieces = [(i, g) for i in range(B) for g in range(4)]
    for n, (i, g) in enumerate(pieces):
        loop(H // 4, lambda k: head(i, g * (H // 4) + k))
        if with_slab and n == 1:
            out_copy.wait()
            fold(out_grads, out_cross)
            for s in order:
                near_out.first(s)
        if with_slab and n == 4:
            for s in order:
                near_out.second(s)
        if with_slab and n == 7:
            for s in order:
                near_out.third(s, out_slab)
        if n in (1, 4, 7):
            advance()

    kv_send[:, 0:DH] = (kv_sum[pl.ds(0, 2 * T), 0:DH] * scale).astype(BF)
    kv_send[:, DH:] = kv_sum[pl.ds(0, 2 * T), DH:].astype(BF)
    returns = []
    for d in (1, 2):
        to = (p.row, lax.rem(p.col - d + 2 * p.Z, 2 * p.Z))
        copy = remote(
            kv_send.at[pl.ds((2 - d) * T, T)], kv_recv.at[d - 1], ksend.at[d - 1], krecv.at[d - 1], to
        )
        pl.when(spot - d >= 0)(copy.start)
        returns.append((d, copy))

    def turn(t):
        query_grad[at(t, BLOCK)] = query_grad_t[:, at(t, BLOCK)].T

    loop(B, turn)

    def query_weight_grad(t):
        put(act_grads, t, slice(0, E), product(attn_in_t[at(t, BLOCK)], query_grad[...]))

    loop(D // BLOCK, query_weight_grad)
    kv_grad[:, 0:DH] = kv_sum[pl.ds(2 * T, T), 0:DH] * scale
    kv_grad[:, DH:] = kv_sum[pl.ds(2 * T, T), DH:]
    for d, copy in returns:
        @pl.when(spot + d < pack)
        def _():
            copy.wait_recv()
            kv_grad[...] += kv_recv[d - 1].astype(F32)

    window[pl.ds(0, T)] = kv_grad[...].astype(BF)

    def keyval_weight_grad(t):
        put(act_grads, t, slice(E, QK), product(attn_in_t[at(t, BLOCK)], window[pl.ds(0, T)]))

    loop(D // BLOCK, keyval_weight_grad)

    def input_grad(t, total):
        rows = at(t, 128)
        grad = against(query_grad[rows], slabs[:, 0:E]) + against(window[rows], slabs[:, E:QK])
        value = tokens[rows].astype(F32)
        scale_first = rms_scale(value)
        total = total + fold_rows(grad * (value * scale_first))
        m = grad * gains[0:1]
        grad_tokens[rows] = grad_in[rows] + scale_first * m - value * (
            scale_first * scale_first * scale_first * jnp.mean(m * value, axis=-1, keepdims=True)
        )
        return total

    total = lax.fori_loop(0, T // 128, input_grad, jnp.zeros((8, D), F32))
    gain_rows[0:1] = jnp.sum(total, axis=0, keepdims=True)

    def gain_grad(t):
        put(act_grads, t, slice(QK, QK + 128), gain_rows[:, at(t, BLOCK)].T)

    loop(D // BLOCK, gain_grad)
    if with_slab:
        act_copy = crossing(act_grads, act_cross, 1)
        act_copy.start()
        act_copy.wait()
        fold(act_grads, act_cross)
        for s in order:
            near_act.first(s)
        for s in order:
            near_act.second(s)
        for s in order:
            near_act.third(s, act_slab)
    else:
        out_slab[...] = out_grads[...]
        act_slab[...] = act_grads[...]
    while ticks:
        advance()
    for d, copy in returns:
        pl.when(spot - d >= 0)(copy.wait_send)
    far.finish()
    if with_slab:
        near_out.finish()
        near_act.finish()


def backward(shape, with_slab, tokens, cot, middle, grad_in, slabs, query, window, bias, att, lse, grads):
    X, Y, Z = sides(shape)
    R = shape[0]
    T, D = tokens.shape
    E, hz = H * DH, grads.shape[2] // 3
    W = slabs.shape[1]
    B = T // BLOCK
    span = WINDOW + BLOCK
    n = scatter_count(X, Y, Z)
    S, V = jax.ShapeDtypeStruct, pltpu.VMEM
    block = (D // R, 3 * hz)
    half = (block[0] // 2, block[1])
    A = E + 2 * DH + 128
    ar = D // (R * Z * 2)
    if with_slab:
        slab_outs = [S((ar, E), F32), S((ar, A), F32)]
        slab_work = [V((R * Z, 2, ar, E), BF), V((R * Z, 2, ar, A), BF)]
    else:
        slab_outs = [S((D, E), BF), S((D, A), BF)]
        slab_work = [V((D, E), BF), V((D, A), BF)]
    outs = [S((T, D), F32), S(block, F32)] + slab_outs
    scratch = [
        V((T, D), BF), V((T, D), BF), V((T, D), F32), V((T, D), F32), V((D, W), BF), V((T, E), BF),
        V((3 * T, 2 * DH), BF), V((B, span, BLOCK), F32), V((E, T), BF), V((H * B, 8, BLOCK), F32),
        V((8, D), F32), V((DH, 3 * T), BF), V((T, D), BF), V((E, T), BF), V((E, T), BF), V((T, E), BF),
        V((3 * T, 2 * DH), F32), V((2 * T, 2 * DH), BF), V((2, T, 2 * DH), BF), V((T, 2 * DH), F32),
        V((D, T), BF), *slab_work, V((128, D), F32),
        V((Z, X - 1) + half, BF), V((Z, Y - 1) + half, BF), V((Z,) + block, BF),
        *scatter_scratch(X, Y, Z, block),
    ]
    if with_slab:
        scratch += [V((R * Z, ar, E), BF), V((R * Z, ar, A), BF)]
        scratch += scatter_scratch(X, Y, Z, (ar, E)) + scatter_scratch(X, Y, Z, (ar, A))
    scratch += [
        DMA((n,)), DMA((n,)), DMA((2,)), DMA((2,)), DMA((10,)), DMA((1,)), DMA((Z * (X + Y - 1),)),
    ]
    if with_slab:
        scratch += [DMA((n,))] * 4 + [DMA((2,))] * 2
    return pl.pallas_call(
        functools.partial(backward_kernel, shape, with_slab, (D, T, E, W, hz)),
        out_shape=outs,
        in_specs=[ANY] * 11,
        out_specs=[VM] * 4,
        scratch_shapes=scratch,
        compiler_params=pltpu.CompilerParams(
            collective_id=1, has_side_effects=True, vmem_limit_bytes=62 << 20
        ),
        name="backward",
    )(tokens, cot, middle, grad_in, slabs, query, window, bias, att, lse, grads)


def shards(
    shape,
    tokens, gain_attn, w_query, w_keyval, w_out, gain_mlp, w_gate, w_up, w_down, segment, cotangent
):
    D = tokens.shape[1]
    with_slab = w_query.shape[0] % 32 == 0
    ffn = jnp.concatenate([w_gate, w_up, w_down.T], axis=1)
    slab = jnp.concatenate(
        [w_query, w_keyval, w_out,
         jnp.pad(jnp.stack([gain_attn, gain_mlp], axis=1), ((0, 0), (0, 126)))], axis=1)
    if not with_slab:
        slab = lax.all_gather(slab, ("row", "col"), axis=0, tiled=True)
    marks = jnp.broadcast_to(segment.astype(F32)[None], (8, segment.shape[0]))
    output, grad_in, middle, *kept = forward(shape, with_slab, tokens, cotangent, marks, slab, ffn)
    grad_tokens, ffn_grad, out_grad, act_grad = backward(
        shape, with_slab, tokens, cotangent, middle, grad_in, *kept)
    if not with_slab:
        out_grad, act_grad = (
            lax.psum_scatter(g.astype(F32), ("row", "col"), scatter_dimension=0, tiled=True)
            for g in (out_grad, act_grad)
        )
    E = H * DH
    hz = w_gate.shape[1]
    return (
        output,
        grad_tokens,
        act_grad[:, E + 2 * DH],
        act_grad[:, :E],
        act_grad[:, E : E + 2 * DH],
        out_grad,
        act_grad[:, E + 2 * DH + 1],
        ffn_grad[:, :hz],
        ffn_grad[:, hz : 2 * hz],
        ffn_grad[:, 2 * hz :].T,
    )


def solution(mesh):
    shape = (mesh.shape["row"], mesh.shape["col"])
    return jax.shard_map(
        functools.partial(shards, shape),
        mesh=mesh,
        in_specs=(
            P(("row", "col"), None),
            P(("row", "col")),
            P(("row", "col"), None),
            P(("row", "col"), None),
            P(("row", "col"), None),
            P(("row", "col")),
            P("row", "col"),
            P("row", "col"),
            P("col", "row"),
            P(("row", "col")),
            P(("row", "col"), None),
        ),
        out_specs=(
            P(("row", "col"), None),
            P(("row", "col"), None),
            P(("row", "col")),
            P(("row", "col"), None),
            P(("row", "col"), None),
            P(("row", "col"), None),
            P(("row", "col")),
            P("row", "col"),
            P("row", "col"),
            P("col", "row"),
        ),
        check_vma=False,
    )
```

profile of v0, /device:TPU:0, one launch (start us, length us, event | category | flops | bytes accessed | tf_op | source)
XLA Modules:
  0.0 321.6 jit_solution(17233740156705131260)
XLA Ops:
  0.6 0.7 pad_maximum_fusion.1
  1.3 0.7 convert_element_type.5
  2.0 0.1 copy.29
  2.1 0.6 broadcast_in_dim.2.refs_2_
  2.7 1.6 fusion.1.refs_3_
  4.3 1.1 copy.30
  5.4 1.9 pad_maximum_fusion.refs_4_
  7.3 150.8 %forward.1 = (bf16[512,1024]{1,0:T(8,128)(2,1)}, f32[512,1024]{1,0:T(8,128)}, f32[512,1024]{1,0:T(8,128)}, bf16[1024,2432]{1,0:T(8,128)(2,1)}, bf16[512,1024]{1,...) custom-call(bf16[512,1024]{1,0:T(8,128)(2,1)} %refs_0_.3, ...), custom_call_target="tpu_custom_call" | custom-call | tf_op jit(solution)/shard_map/forward/pallas_call | solution.py:608
  158.1 152.8 %backward.1 = (f32[512,1024]{1,0:T(8,128)}, f32[256,1152]{1,0:T(8,128)}, f32[32,1024]{1,0:T(8,128)}, f32[32,1408]{1,0:T(8,128)}) custom-call(bf16[512,1024]{1,0:T(8,128)(2,1)} %refs_0_.3, bf16[512,1024]{1,0:T(8,128)(2,1)} %refs_1_.3, f32[512,1024]{1,0:T(8,128)} %get-tuple-element.25.refs_2_, f32[512,1024]{1,0:T(8,128)} %get-tuple-element.26.refs_3_, ...), custom_call_target="tpu_custom_call" | custom-call | tf_op jit(solution)/shard_map/backward/pallas_call | solution.py:954
  310.9 0.0 copy-start.1
  310.9 1.5 slice_reduce_fusion
  312.5 1.4 slice.23
  313.8 1.6 slice.22
  315.4 0.0 copy-start
  315.4 2.3 slice_bitcast_fusion
  317.7 0.9 copy.31
  318.6 0.0 copy-done.1
  318.6 1.0 copy.35
  319.6 0.0 copy-done
  319.6 0.0 copy-start.2
  319.6 1.3 copy.36
  320.9 0.0 copy-done.2
  320.9 0.7 copy.37
Async XLA Ops:
  310.9 7.7 %copy-start.1 = (bf16[512,1024]{1,0:T(8,128)(2,1)S(1)}, bf16[512,1024]{1,0:T(8,128)(2,1)}, u32[]{:S(2)}) copy-start(bf16[512,1024]{1,0:T(8,128)(2,1)} %get-tuple-element.83) | copy-start | bytes 3145732
  315.4 4.2 %copy-start = (f32[512,1024]{1,0:T(8,128)S(1)}, f32[512,1024]{1,0:T(8,128)}, u32[]{:S(2)}) copy-start(f32[512,1024]{1,0:T(8,128)} %get-tuple-element.84) | copy-start | bytes 6291460
  319.6 1.3 copy-start.2
where the time goes:
time: 322 us
  Pallas kernels  304 us (94%)
  local copies, waits for them, and re-layouts  12.5 us (4%)
  other arithmetic  4.82 us (1%)
    pallas_call x1, Pallas kernels, backward(): pl.pallas_call(functools.partial(backward_kernel, shape, with_slab, (D, T...  153 us
    pallas_call x1, Pallas kernels, forward(): pl.pallas_call(functools.partial(forward_kernel, shape, with_slab, (D, T,...  151 us

commit v1 on v0

v1 whole, which is shorter than its diff:
```python
import functools
import math

import jax
import jax.numpy as jnp
from jax import lax
from jax.experimental import pallas as pl
from jax.experimental.pallas import tpu as pltpu
from jax.sharding import PartitionSpec as P

H = 8
DH = 128
WINDOW = 1024
PACK = 2048

EPS = 1e-06
NEGATIVE = -1e30
MESH = pl.DeviceIdType.MESH
BF = jnp.bfloat16
F32 = jnp.float32


def product(left, right):
    return jnp.dot(left, right, preferred_element_type=jnp.float32)


def inner(left, right):
    return lax.dot_general(
        left, right, (((0,), (0,)), ((), ())), preferred_element_type=jnp.float32
    )


def against(left, right):
    return lax.dot_general(
        left, right, (((1,), (1,)), ((), ())), preferred_element_type=jnp.float32
    )


class Place:
    def __init__(self, shape):
        rows, cols = shape
        self.X = math.isqrt(rows)
        while rows % self.X:
            self.X -= 1
        self.Y = rows // self.X
        self.Z = cols // 2
        self.R = rows
        self.row, self.col = lax.axis_index("row"), lax.axis_index("col")
        self.y, self.x = self.row // self.X, self.row % self.X
        self.z, self.core = self.col // 2, self.col % 2
        self.xs, self.ys, self.zs = range(1, self.X), range(1, self.Y), range(1, self.Z)

    def row_at(self, dy=0, dx=0):
        return lax.rem(self.y + dy + self.Y, self.Y) * self.X + lax.rem(
            self.x + dx + self.X, self.X
        )

    def z_at(self, dz):
        return lax.rem(self.z + dz + self.Z, self.Z)

    def device(self, dy=0, dx=0, dz=0, other=False):
        core = 1 - self.core if other else self.core
        return (self.row_at(dy, dx), self.z_at(dz) * 2 + core)


def remote(src, dst, send, recv, device):
    return pltpu.make_async_remote_copy(
        src_ref=src, dst_ref=dst, send_sem=send, recv_sem=recv, device_id=device,
        device_id_type=MESH,
    )


class Sems:
    def __init__(self, send, recv):
        self.send, self.recv, self.count = send, recv, 0

    def take(self):
        self.count += 1
        return self.send.at[self.count - 1], self.recv.at[self.count - 1]


def gather_count(X, Y, K):
    return (K - 1) + K * ((X - 1) + (Y - 1) + 2 * (X - 1) * (Y - 1))


class Gather:
    def __init__(self, at, dest, here, sems, own, stride=1):
        self.at, self.dest, self.p, self.own = at, dest, here, own
        self.stride, self.K = stride, here.Z // stride
        self.sent = []
        p = here
        self.zsem = {k: sems.take() for k in range(1, self.K)}
        self.xsem = {(s, d): sems.take() for s in range(self.K) for d in p.xs}
        self.ysem = {(s, d): sems.take() for s in range(self.K) for d in p.ys}
        self.dsem = {
            (s, h, dx, dy): sems.take()
            for s in range(self.K) for h in (0, 1) for dx in p.xs for dy in p.ys
        }

    def push(self, src, dst, sem, device):
        copy = remote(src, dst, sem[0], sem[1], device)
        copy.start()
        self.sent.append(copy)

    def arrive(self, place, sem):
        remote(place, place, sem[0], sem[1], self.p.device(other=True)).wait_recv()

    def spread_z(self):
        p = self.p
        for k in range(1, self.K):
            self.push(self.own, self.dest(k), self.zsem[k], p.device(dz=-self.stride * k))

    def spread_xy(self, s):
        if s >= self.K:
            return
        p = self.p
        place = self.at(s, p.row, None)
        src = self.own
        if s:
            self.arrive(place, self.zsem[s])
            src = place
        for d in p.xs:
            self.push(src, place, self.xsem[s, d], p.device(dx=d))
        for d in p.ys:
            self.push(src, place, self.ysem[s, d], p.device(dy=d))

    def spread_diagonal(self, s):
        if s >= self.K:
            return
        p = self.p
        for d in p.xs:
            r = p.row_at(dx=-d)
            self.arrive(self.at(s, r, None), self.xsem[s, d])
            half = self.at(s, r, 0)
            for e in p.ys:
                self.push(half, half, self.dsem[s, 0, d, e], p.device(dy=e))
        for e in p.ys:
            r = p.row_at(dy=-e)
            self.arrive(self.at(s, r, None), self.ysem[s, e])
            half = self.at(s, r, 1)
            for d in p.xs:
                self.push(half, half, self.dsem[s, 1, d, e], p.device(dx=d))

    def close(self, s):
        p = self.p
        for d in p.xs:
            for e in p.ys:
                r = p.row_at(dy=-e, dx=-d)
                for h in (0, 1):
                    self.arrive(self.at(s, r, h), self.dsem[s, h, d, e])

    def finish(self):
        for copy in self.sent:
            copy.wait_send()


def scatter_count(X, Y, K):
    return (K - 1) + K * (2 * (X - 1) * (Y - 1) + 2 * (X - 1) + 2 * (Y - 1))


class Scatter:
    def __init__(
        self, part, cut, here, sems, termx, termy, own, diag, fromx, fromy, fromz, stride=1
    ):
        self.part, self.cut, self.p = part, cut, here
        self.termx, self.termy, self.own = termx, termy, own
        self.diag, self.fromx, self.fromy, self.fromz = diag, fromx, fromy, fromz
        self.stride, self.K = stride, here.Z // stride
        self.sent = []
        p = here
        self.zsem = {k: sems.take() for k in range(1, self.K)}
        self.xsem = {(s, h, d): sems.take() for s in range(self.K) for h in (0, 1) for d in p.xs}
        self.ysem = {(s, h, d): sems.take() for s in range(self.K) for h in (0, 1) for d in p.ys}
        self.dsem = {
            (s, h, dx, dy): sems.take()
            for s in range(self.K) for h in (0, 1) for dx in p.xs for dy in p.ys
        }

    def push(self, src, dst, sem, device):
        copy = remote(src, dst, sem[0], sem[1], device)
        copy.start()
        self.sent.append(copy)

    def arrive(self, place, sem):
        remote(place, place, sem[0], sem[1], self.p.device(other=True)).wait_recv()

    def spot(self, d, e):
        return (d - 1) * (self.p.Y - 1) + e - 1

    def first(self, s):
        p, cut = self.p, self.cut
        for d in p.xs:
            for e in p.ys:
                far = self.part(s, p.row_at(dy=e, dx=d))
                n = self.spot(d, e)
                self.push(cut(far, 0), self.diag.at[s, 0, n], self.dsem[s, 0, d, e], p.device(dx=d))
                self.push(cut(far, 1), self.diag.at[s, 1, n], self.dsem[s, 1, d, e], p.device(dy=e))
        for d in p.xs:
            near = self.part(s, p.row_at(dx=d))
            self.push(cut(near, 0), cut(self.fromx.at[s, d - 1], 0), self.xsem[s, 0, d], p.device(dx=d))
        for e in p.ys:
            near = self.part(s, p.row_at(dy=e))
            self.push(cut(near, 1), cut(self.fromy.at[s, e - 1], 1), self.ysem[s, 1, e], p.device(dy=e))

    def second(self, s):
        p, cut = self.p, self.cut
        for e in p.ys:
            term = self.termy(s, e)
            total = term[...].astype(F32)
            for d in p.xs:
                place = self.diag.at[s, 0, self.spot(d, e)]
                self.arrive(place, self.dsem[s, 0, d, e])
                total = total + place[...].astype(F32)
            term[...] = total.astype(BF)
            self.push(term, cut(self.fromy.at[s, e - 1], 0), self.ysem[s, 0, e], p.device(dy=e))
        for d in p.xs:
            term = self.termx(s, d)
            total = term[...].astype(F32)
            for e in p.ys:
                place = self.diag.at[s, 1, self.spot(d, e)]
                self.arrive(place, self.dsem[s, 1, d, e])
                total = total + place[...].astype(F32)
            term[...] = total.astype(BF)
            self.push(term, cut(self.fromx.at[s, d - 1], 1), self.xsem[s, 1, d], p.device(dx=d))

    def third(self, s, out=None):
        p, cut = self.p, self.cut
        own = self.own(s)
        total = own[...].astype(F32)
        for d in p.xs:
            for h in (0, 1):
                self.arrive(cut(self.fromx.at[s, d - 1], h), self.xsem[s, h, d])
            total = total + self.fromx[s, d - 1].astype(F32)
        for e in p.ys:
            for h in (0, 1):
                self.arrive(cut(self.fromy.at[s, e - 1], h), self.ysem[s, h, e])
            total = total + self.fromy[s, e - 1].astype(F32)
        if s:
            own[...] = total.astype(BF)
            self.push(own, self.fromz.at[s - 1], self.zsem[s], p.device(dz=self.stride * s))
            return
        for k in range(1, self.K):
            self.arrive(self.fromz.at[k - 1], self.zsem[k])
            total = total + self.fromz[k - 1].astype(F32)
        out[...] = total

    def finish(self):
        for copy in self.sent:
            copy.wait_send()


def scatter_scratch(X, Y, K, block):
    half = (block[0] // 2, block[1])
    return [
        pltpu.VMEM((K, 2, (X - 1) * (Y - 1)) + half, BF),
        pltpu.VMEM((K, X - 1) + block, BF),
        pltpu.VMEM((K, Y - 1) + block, BF),
        pltpu.VMEM((max(K - 1, 1),) + block, BF),
    ]


def sides(shape):
    x = math.isqrt(shape[0])
    while shape[0] % x:
        x -= 1
    return x, shape[0] // x, shape[1] // 2


VM = pl.BlockSpec(memory_space=pltpu.VMEM)
ANY = pl.BlockSpec(memory_space=pl.ANY)
DMA = pltpu.SemaphoreType.DMA
LOG2E = math.log2(math.e)
BLOCK = 256


def loop(count, body):
    def step(t, carry):
        body(t)
        return carry

    lax.fori_loop(0, count, step, 0)


def at(t, size):
    return pl.ds(pl.multiple_of(t * size, size), size)


def rms_scale(value):
    return lax.rsqrt(jnp.mean(value * value, axis=-1, keepdims=True) + EPS)


def gelu_parts(gate):
    square = gate * gate
    t = jnp.tanh(gate * (0.7978845608 + (0.7978845608 * 0.044715) * square))
    half = 0.5 + 0.5 * t
    slope = half + (0.5 * gate) * (1.0 - t * t) * (
        0.7978845608 + (3 * 0.7978845608 * 0.044715) * square
    )
    return gate * half, slope


class Pack:
    def __init__(self, here, T):
        p = here
        self.p, self.size = p, PACK // T
        self.spot = lax.rem(p.col, self.size)
        pair = (p.z // 2) * 2 + 1 - lax.rem(p.z, 2)
        self.mate = p.device(other=True)
        self.pair = (p.row, pair * 2 + p.core)
        self.across = (p.row, pair * 2 + 1 - p.core)

    def greet(self):
        p = self.p
        barrier = pltpu.get_barrier_semaphore()
        mates = [p.device(dx=d) for d in p.xs] + [p.device(dy=d) for d in p.ys]
        mates += [p.device(dz=d) for d in p.zs] + [self.mate, self.across]
        for mate in mates:
            pl.semaphore_signal(barrier, inc=1, device_id=mate, device_id_type=MESH)
        return lambda: pl.semaphore_wait(barrier, len(mates))


def slab_lanes():
    E, QK = H * DH, H * DH + 2 * DH
    return E, QK, QK + 128


def forward_kernel(shape, with_slab, sizes, *refs):
    D, T, W, hz = sizes
    (tokens, cot, marks, slab, ffn,
     grad_in, middle, out_own, out_far, slabs_out, query_out, window_out, bias_out, att_out, lse_out, grads_out,
     slabs, ffns, query, window, values_t, marks_all, bias, att, lse, gains, mlp, cots,
     grad_tile, out_tile, hidden, grad_act, side_grad, side_out, cross_grad, cross_out, far_grad,
     mate_grad, mate_out, pre_grad, pre_out, pair_grad,
     asend, arecv, osend, orecv, fsend, frecv, csend, crecv, ksend, krecv, tsend, trecv, msend, mrecv,
     gsend, grecv, lsem, gsem) = refs
    p = Place(shape)
    pack = Pack(p, T)
    mate, pair, spot = pack.mate, pack.pair, pack.spot
    E, QK, WO = slab_lanes()
    B = T // BLOCK
    span = WINDOW + BLOCK
    K = p.Z // 2

    def local(src, dst, n):
        copy = pltpu.make_async_copy(src, dst, lsem.at[n])
        copy.start()
        return copy

    ready = pack.greet()
    load_cot = local(cot, cots.at[pl.ds(0, T)], 0)
    if not with_slab:
        load_slab = local(slab, slabs, 1)
    ready()

    br = ffn.shape[0]

    def ffn_at(s, r, half):
        if half is None:
            return ffns.at[s, at(r, br)]
        return ffns.at[s, pl.ds(pl.multiple_of(r * br + half * (br // 2), br // 2), br // 2)]

    far = Gather(ffn_at, lambda k: ffn_at(k, p.row, None), p, Sems(fsend, frecv), ffn, 2)

    if with_slab:
        ar = slab.shape[0]

        def slab_place(lanes, core):
            def place(s, r, half):
                start = ((r * p.Z + p.z_at(s)) * 2 + core) * ar
                if half is None:
                    return slabs.at[pl.ds(pl.multiple_of(start, ar), ar), lanes]
                start = pl.multiple_of(start + half * (ar // 2), ar // 2)
                return slabs.at[pl.ds(start, ar // 2), lanes]

            return place

        def slab_gather(lanes, sems):
            place = slab_place(lanes, p.core)
            return Gather(place, lambda k: place(0, p.row, None), p, sems, slab.at[:, lanes])

        act_lanes, out_lanes = slice(0, WO), slice(WO, W)
        near = slab_gather(act_lanes, Sems(asend, arecv))
        near_out = slab_gather(out_lanes, Sems(osend, orecv))
        hands = Sems(csend, crecv)

        def hand(gather, lanes):
            mine, theirs = slab_place(lanes, p.core), slab_place(lanes, 1 - p.core)
            passed = []
            for s in range(p.Z):
                gather.close(s)
                for dy in range(p.Y):
                    for dx in range(p.X):
                        r = p.row_at(dy, dx)
                        send, recv = hands.take()
                        place, other = mine(s, r, None), theirs(s, r, None)
                        copy = remote(place, place, send, recv, mate)
                        copy.start()
                        passed.append((copy, remote(other, other, send, recv, mate)))
            return passed

        near.spread_z()
        near.spread_xy(0)
        near_out.spread_z()

    marks_all[:, pl.ds(2 * T, T)] = marks[...]

    @pl.when(spot == 0)
    def _():
        window[pl.ds(0, 2 * T), :] = jnp.zeros((2 * T, 2 * DH), BF)
        marks_all[:, pl.ds(0, 2 * T)] = jnp.full((8, 2 * T), -1.0, F32)

    @pl.when(spot == 1)
    def _():
        window[pl.ds(0, T), :] = jnp.zeros((T, 2 * DH), BF)
        marks_all[:, pl.ds(0, T)] = jnp.full((8, T), -1.0, F32)

    def behind(src, place, n, op):
        for d in (1, 2):
            to = (p.row, lax.rem(p.col + d, 2 * p.Z))
            copy = remote(src, place(2 - d), ksend.at[n + d], krecv.at[n + d], to)
            if op == "start":
                pl.when(spot + d < pack.size)(copy.start)
            elif op == "arrive":
                pl.when(spot - d >= 0)(copy.wait_recv)
            else:
                pl.when(spot + d < pack.size)(copy.wait_send)

    mark_place = lambda k: marks_all.at[:, pl.ds(k * T, T)]
    mark_own = mark_place(2)
    behind(mark_own, mark_place, 0, "start")

    def whole(ref, n):
        return ref.at[pl.ds(n * T, T)]

    load_cot.wait()
    cot_mate = remote(whole(cots, 0), whole(cots, 1), tsend.at[0], trecv.at[0], mate)
    cot_pair = remote(whole(cots, 0), whole(cots, 2), tsend.at[1], trecv.at[1], pair)
    cot_pass = remote(whole(cots, 2), whole(cots, 3), tsend.at[2], trecv.at[2], mate)
    cot_mate.start()
    if with_slab:
        slabs[pl.ds(pl.multiple_of(((p.row * p.Z + p.z) * 2 + p.core) * ar, ar), ar)] = slab[...]
    ffns[0, at(p.row, br)] = ffn[...]
    if with_slab:
        for s in range(p.Z):
            near.spread_xy(s + 1)
            if s == 0:
                near_out.spread_xy(0)
            near.spread_diagonal(s)
        far.spread_z()
        cot_pair.start()
        for s in range(1, p.Z):
            near_out.spread_xy(s)
        passed = hand(near, act_lanes)
        far.spread_xy(0)
        for s in range(p.Z):
            near_out.spread_diagonal(s)
        for copy, arrival in passed:
            copy.wait_send()
            arrival.wait_recv()
    else:
        far.spread_z()
        cot_pair.start()
        far.spread_xy(0)
        load_slab.wait()
    gains[...] = slabs[:, QK:WO].astype(F32).T[0:8]

    def first_norm(t):
        rows = at(t, 64)
        value = tokens[rows].astype(F32)
        mlp[rows] = (value * rms_scale(value) * gains[0:1]).astype(BF)

    loop(T // 64, first_norm)
    window[pl.ds(2 * T, T)] = product(mlp[pl.ds(0, T)], slabs[:, E:QK]).astype(BF)
    key_place = lambda k: window.at[pl.ds(k * T, T)]
    behind(key_place(2), key_place, 3, "start")

    def project(t):
        query[at(t, BLOCK)] = product(mlp[at(t, BLOCK)], slabs[:, 0:E]).astype(BF)

    loop(B, project)
    save_query = local(query, query_out, 2)
    if with_slab:
        passed = hand(near_out, out_lanes)
    behind(mark_own, mark_place, 0, "arrive")
    column = jnp.broadcast_to(marks_all[0:1], (128, 3 * T)).T
    for i in range(B):
        keys_at = jnp.concatenate([column[i * BLOCK : i * BLOCK + span]] * (BLOCK // 128), axis=1)
        own = marks_all[0:1, 2 * T + i * BLOCK : 2 * T + (i + 1) * BLOCK]
        gap = (
            WINDOW
            + lax.broadcasted_iota(jnp.int32, (span, BLOCK), 1)
            - lax.broadcasted_iota(jnp.int32, (span, BLOCK), 0)
        )
        allowed = (keys_at == own) & (gap >= 0) & (gap < WINDOW)
        bias[i] = jnp.where(allowed, 0.0, NEGATIVE)
    save_bias = local(bias, bias_out, 3)
    behind(key_place(2), key_place, 3, "arrive")
    save_window = local(window, window_out, 4)
    values_t[...] = window[:, DH:].T
    factor = LOG2E / math.sqrt(DH)

    def head(i, h):
        lanes = at(h, DH)
        keys = window[pl.ds(i * BLOCK, span), 0:DH]
        scores = against(keys, query[pl.ds(i * BLOCK, BLOCK), lanes]) * factor + bias[i]
        top = jnp.max(scores, axis=0, keepdims=True)
        expo = jnp.exp2(scores - top)
        total = jnp.sum(expo, axis=0, keepdims=True)
        mixed = product(values_t[:, pl.ds(i * BLOCK, span)], expo.astype(BF))
        att[lanes, pl.ds(i * BLOCK, BLOCK)] = (mixed / total).astype(BF)
        lse[h * B + i] = jnp.broadcast_to(top + jnp.log2(total), (8, BLOCK))

    def tile_of(ref, n, i):
        return ref.at[pl.ds(pl.multiple_of(n * T + i * BLOCK, BLOCK), BLOCK)]

    def mlp_copy(n, i):
        to = pair if n == 2 else mate
        src = 2 if n == 3 else 0
        sem = (n - 1) * B + i
        return remote(tile_of(mlp, src, i), tile_of(mlp, n, i), msend.at[sem], mrecv.at[sem], to)

    for i in range(B):
        if i == 0:
            loop(H // 2, lambda h: head(i, h))
            far.spread_xy(1)
            far.spread_diagonal(0)
            loop(H // 2, lambda h: head(i, h + H // 2))
            if with_slab:
                for copy, arrival in passed:
                    copy.wait_send()
                    arrival.wait_recv()
            save_slabs = local(slabs, slabs_out, 1)
        else:
            loop(H, lambda h: head(i, h))
        cols = pl.ds(i * BLOCK, BLOCK)
        middle[cols] = product(att[:, cols].T, slabs[:, WO:]) + tokens[cols].astype(F32)

        def second_norm(t):
            rows = pl.ds(pl.multiple_of(i * BLOCK + t * 64, 64), 64)
            value = middle[rows]
            mlp[rows] = (value * rms_scale(value) * gains[1:2]).astype(BF)

        loop(BLOCK // 64, second_norm)
        mlp_copy(1, i).start()
        mlp_copy(2, i).start()
        if i == 0:
            cot_pair.wait_recv()
            cot_pass.start()
    save_att = local(att, att_out, 5)
    save_lse = local(lse, lse_out, 6)
    for s in range(2, K):
        far.spread_xy(s)
    for s in range(1, K):
        far.spread_diagonal(s)
    mlp_copy(2, 0).wait_recv()
    mlp_copy(3, 0).start()
    for s in range(K):
        far.close(s)
    cot_mate.wait()
    cot_pass.wait_recv()

    def grad_copy(i):
        return [
            remote(tile_of(side_grad, 0, i), tile_of(mate_grad, 0, i), gsend.at[i], grecv.at[i], mate),
            remote(tile_of(side_out, 0, i), tile_of(mate_out, 0, i), gsend.at[B + i], grecv.at[B + i], mate),
        ]

    def cross_copy(i):
        n = 2 * B
        return [
            remote(tile_of(cross_grad, 0, i), tile_of(pre_grad, 0, i), gsend.at[n + i], grecv.at[n + i], mate),
            remote(tile_of(cross_out, 0, i), tile_of(pre_out, 0, i), gsend.at[n + B + i], grecv.at[n + B + i], mate),
        ]

    def far_copy(i):
        n = 4 * B + i
        return remote(tile_of(far_grad, 0, i), tile_of(pair_grad, 0, i), gsend.at[n], grecv.at[n], pair)

    def feed(t):
        i, kind = t // 4, lax.rem(t, 4)
        n = jnp.where(kind == 2, 3, jnp.where(kind == 3, 2, kind))

        @pl.when(kind == 1)
        def _():
            mlp_copy(1, i).wait_recv()

        @pl.when(kind == 2)
        def _():
            mlp_copy(3, i).wait_recv()

        rows = pl.ds(pl.multiple_of(n * T + i * BLOCK, BLOCK), BLOCK)
        for s in range(K):
            gate_up = product(mlp[rows], ffns[s, :, 0 : 2 * hz])
            grad_hidden = product(cots[rows], ffns[s, :, 2 * hz :])
            up = gate_up[:, hz:]
            act, slope = gelu_parts(gate_up[:, :hz])
            hidden[s, rows] = (act * up).astype(BF)
            grad_act[s, rows, 0:hz] = (grad_hidden * up * slope).astype(BF)
            grad_act[s, rows, hz : 2 * hz] = (grad_hidden * act).astype(BF)
            outs = against(hidden[s, rows], ffns[s, :, 2 * hz :])
            grads = against(grad_act[s, rows], ffns[s, :, 0 : 2 * hz])
            if s == 0:
                out_tile[...] = outs
                grad_tile[...] = grads
            else:
                out_tile[...] += outs
                grad_tile[...] += grads
        here = pl.ds(pl.multiple_of(i * BLOCK, BLOCK), BLOCK)

        @pl.when(kind == 0)
        def _():
            grad_in[here] = grad_tile[...]
            out_own[here] = middle[here] + out_tile[...]

        @pl.when(kind == 1)
        def _():
            side_grad[here] = grad_tile[...].astype(BF)
            side_out[here] = out_tile[...].astype(BF)
            for copy in grad_copy(i):
                copy.start()

        @pl.when(kind == 2)
        def _():
            cross_grad[here] = grad_tile[...].astype(BF)
            cross_out[here] = out_tile[...].astype(BF)
            for copy in cross_copy(i):
                copy.start()

        @pl.when(kind == 3)
        def _():
            for copy in cross_copy(i):
                copy.wait_recv()
            far_grad[here] = (grad_tile[...] + pre_grad[here].astype(F32)).astype(BF)
            out_far[here] = (out_tile[...] + pre_out[here].astype(F32)).astype(BF)
            far_copy(i).start()

    loop(4, feed)
    for i in range(1, B):
        mlp_copy(2, i).wait_recv()
        mlp_copy(3, i).start()
        loop(4, lambda t: feed(t + 4 * i))

    far.finish()

    def weight_tile(t):
        rows = at(t, BLOCK)
        for s in range(K):
            ffns[s, rows, 0 : 2 * hz] = inner(mlp[:, rows], grad_act[s]).astype(BF)
            ffns[s, rows, 2 * hz :] = inner(cots[:, rows], hidden[s]).astype(BF)

    loop(D // BLOCK, weight_tile)
    save_grads = pltpu.make_async_copy(ffns, grads_out, gsem.at[0])
    save_grads.start()

    def join(t):
        rows = at(t, 64)
        out_own[rows] = out_own[rows] + mate_out[rows].astype(F32)
        grad_in[rows] = grad_in[rows] + mate_grad[rows].astype(F32) + pair_grad[rows].astype(F32)

    for i in range(B):
        for copy in grad_copy(i):
            copy.wait()
        for copy in cross_copy(i):
            copy.wait_send()
        far_copy(i).wait()
        for n in (1, 2, 3):
            mlp_copy(n, i).wait_send()
    loop(T // 64, join)
    for save in (save_slabs, save_query, save_bias, save_window, save_att, save_lse, save_grads):
        save.wait()
    behind(mark_own, mark_place, 0, "sent")
    behind(key_place(2), key_place, 3, "sent")
    cot_pair.wait_send()
    cot_pass.wait_send()
    if with_slab:
        near.finish()
        near_out.finish()


def forward(shape, with_slab, tokens, cot, marks, slab, ffn):
    X, Y, Z = sides(shape)
    R = shape[0]
    T, D = tokens.shape
    E, hz = H * DH, ffn.shape[1] // 3
    W = slab.shape[1]
    B = T // BLOCK
    span = WINDOW + BLOCK
    K = Z // 2
    S, V = jax.ShapeDtypeStruct, pltpu.VMEM
    outs = [
        S((T, D), F32), S((T, D), F32), S((T, D), F32), S((T, D), BF),
        S((D, W), BF), S((T, E), BF), S((3 * T, 2 * DH), BF), S((B, span, BLOCK), F32),
        S((E, T), BF), S((H * B, 8, BLOCK), F32), S((K, D, 3 * hz), BF),
    ]
    near, far = gather_count(X, Y, Z), gather_count(X, Y, K)
    scratch = [
        V((D, W), BF), V((K, D, 3 * hz), BF), V((T, E), BF), V((3 * T, 2 * DH), BF),
        V((DH, 3 * T), BF), V((8, 3 * T), F32), V((B, span, BLOCK), F32), V((E, T), BF),
        V((H * B, 8, BLOCK), F32), V((8, D), F32), V((4 * T, D), BF), V((4 * T, D), BF),
        V((BLOCK, D), F32), V((BLOCK, D), F32), V((K, 4 * T, hz), BF), V((K, 4 * T, 2 * hz), BF),
        *[V((T, D), BF)] * 10,
        *[DMA((near,))] * 4, *[DMA((far,))] * 2, *[DMA((2 * R * Z,))] * 2, *[DMA((6,))] * 2,
        *[DMA((3,))] * 2, *[DMA((3 * B,))] * 2, *[DMA((5 * B,))] * 2, DMA((7,)), DMA((1,)),
    ]
    return pl.pallas_call(
        functools.partial(forward_kernel, shape, with_slab, (D, T, W, hz)),
        out_shape=outs,
        in_specs=[VM, ANY, VM, VM if with_slab else ANY, VM],
        out_specs=[VM] * 4 + [ANY] * 7,
        scratch_shapes=scratch,
        compiler_params=pltpu.CompilerParams(
            collective_id=0, has_side_effects=True, vmem_limit_bytes=62 << 20
        ),
        name="forward",
    )(tokens, cot, marks, slab, ffn)


def backward_kernel(shape, with_slab, sizes, *refs):
    D, T, W, hz = sizes
    E, QK, WO = slab_lanes()
    B = T // BLOCK
    span = WINDOW + BLOCK
    refs = list(refs)

    def some(n):
        taken = refs[:n]
        del refs[:n]
        return taken

    (tokens_in, cot_in, grad_in_in, middle_in, out_own_in, out_far,
     slabs_in, query_in, window_in, bias_in, att_in, lse_in, grads) = some(13)
    output, grad_tokens, ffn_out, out_slab, query_slab, rest_slab = some(6)
    (tokens, cot, middle, grad_in, slabs, query, window, bias, att, lse, out_own, out_pair,
     gains, keys_t, branch, att_grad, query_grad_t, query_grad, kv_sum, kv_send, kv_recv, kv_grad, attn_in_t,
     gain_rows, termx, termy, own) = some(27)
    weight_grads = some(3)
    fwork = some(4)
    if with_slab:
        crossed = some(3)
        works = [some(4) for _ in range(3)]
    fsend, frecv, ksend, krecv, lsem, tsem = some(6)
    if with_slab:
        nsems = some(6)
        xsend, xrecv = some(2)
    p = Place(shape)
    pack = Pack(p, T)
    mate, spot = pack.mate, pack.spot
    K = p.Z // 2
    br = D // p.R

    def part(s, r):
        return grads.at[s, at(r, br)]

    def cut(ref, h):
        rows = ref.shape[0] // 2
        return ref.at[pl.ds(h * rows, rows)]

    ready = pack.greet()
    order = list(range(1, K)) + [0]
    terms = {}
    for s in order:
        copies = []
        for d in p.xs:
            copies.append((cut(part(s, p.row_at(dx=d)), 1), termx.at[s, d - 1]))
        for e in p.ys:
            copies.append((cut(part(s, p.row_at(dy=e)), 0), termy.at[s, e - 1]))
        copies.append((part(s, p.row), own.at[s]))
        n = s * (p.X + p.Y - 1)
        terms[s] = [
            pltpu.make_async_copy(a, b, tsem.at[n + i]) for i, (a, b) in enumerate(copies)
        ]
    pairs = [
        (middle_in, middle), (grad_in_in, grad_in), (cot_in, cot), (slabs_in, slabs), (att_in, att),
        (tokens_in, tokens), (window_in, window), (query_in, query), (bias_in, bias), (lse_in, lse),
        (out_own_in, out_own),
    ]
    loads = [pltpu.make_async_copy(a, b, lsem.at[n]) for n, (a, b) in enumerate(pairs)]
    for load in loads:
        load.start()
    for s in order:
        for copy in terms[s]:
            copy.start()
    ready()
    far = Scatter(
        part, cut, p, Sems(fsend, frecv),
        lambda s, d: termx.at[s, d - 1], lambda s, e: termy.at[s, e - 1], lambda s: own.at[s],
        *fwork, 2
    )
    ticks = []
    for j in range(K + 1):
        tick = []
        if j >= 1:
            tick.append(("third", order[j - 1]))
        if j < K:
            tick.append(("second", order[j]))
        if j + 2 < K:
            tick.append(("first", order[j + 2]))
        ticks.append(tick)

    def advance():
        if ticks:
            for step, s in ticks.pop(0):
                if step == "first":
                    far.first(s)
                elif step == "second":
                    for copy in terms[s]:
                        copy.wait()
                    far.second(s)
                else:
                    far.third(s, ffn_out)

    for s in order[:2]:
        far.first(s)
    out_copy = remote(out_far, out_pair, ksend.at[2], krecv.at[2], pack.pair)
    out_copy.start()

    for load in loads[:4]:
        load.wait()
    gains[...] = slabs[:, QK:WO].astype(F32).T[0:8]
    gain_rows[...] = jnp.zeros_like(gain_rows)

    def fold_rows(value):
        return jnp.sum(value.reshape(value.shape[0] // 8, 8, D), axis=0)

    def second_norm(t, total):
        rows = at(t, 64)
        value, grad = middle[rows], grad_in[rows]
        scale = rms_scale(value)
        total = total + fold_rows(grad * (value * scale))
        n = grad * gains[1:2]
        out = cot[rows].astype(F32) + scale * n - value * (
            scale * scale * scale * jnp.mean(n * value, axis=-1, keepdims=True)
        )
        grad_in[rows] = out
        branch[rows] = out.astype(BF)
        return total

    total = lax.fori_loop(0, T // 64, second_norm, jnp.zeros((8, D), F32))
    gain_rows[1:2] = jnp.sum(total, axis=0, keepdims=True)

    def attended_grad(t):
        att_grad[at(t, BLOCK)] = against(slabs[at(t, BLOCK), WO:], branch[...]).astype(BF)

    loop(E // BLOCK, attended_grad)
    loads[4].wait()
    ar = D // (p.R * p.Z * 2)
    blocks = BLOCK // (2 * ar)

    def put(ref, t, lanes, value):
        if with_slab:
            ref[pl.ds(t * blocks, blocks), :, :, lanes] = value.astype(BF).reshape(
                blocks, 2, ar, value.shape[1]
            )
        else:
            ref[at(t, BLOCK), lanes] = value.astype(BF)

    def out_weight_grad(t):
        put(weight_grads[0], t, slice(0, E), product(att[at(t, BLOCK)], branch[...]))

    loop(E // BLOCK, out_weight_grad)

    class Near:
        def __init__(self, n):
            self.n, self.ref = n, weight_grads[n]
            self.copy = remote(
                self.ref.at[:, 1 - p.core], crossed[n], xsend.at[n], xrecv.at[n], mate
            )
            self.copy.start()

        def block(self, s, r):
            return self.ref.at[r * p.Z + p.z_at(s), p.core]

        def fold(self):
            self.copy.wait()
            ref, other = self.ref, crossed[self.n]

            def step(n):
                ref[n, p.core] = (ref[n, p.core].astype(F32) + other[n].astype(F32)).astype(BF)

            loop(p.R * p.Z, step)
            block = self.block
            self.scatter = Scatter(
                block, cut, p, Sems(*nsems[2 * self.n : 2 * self.n + 2]),
                lambda s, d: cut(block(s, p.row_at(dx=d)), 1),
                lambda s, e: cut(block(s, p.row_at(dy=e)), 0),
                lambda s: block(s, p.row), *works[self.n]
            )
            for s in self.order():
                self.scatter.first(s)

        def order(self):
            return list(range(1, p.Z)) + [0]

        def second(self):
            for s in self.order():
                self.scatter.second(s)

        def third(self):
            for s in self.order()[:-1]:
                self.scatter.third(s)

        def last(self, out):
            self.scatter.third(0, out)
            self.scatter.finish()

    if with_slab:
        near_out = Near(0)

    for load in loads[5:]:
        load.wait()

    def first_norm(t):
        cols = at(t, 128)
        value = tokens[cols].astype(F32)
        attn_in_t[:, cols] = (value * rms_scale(value) * gains[0:1]).astype(BF).T

    loop(T // 128, first_norm)
    keys_t[...] = window[:, 0:DH].T
    kv_sum[...] = jnp.zeros_like(kv_sum)
    if with_slab:
        near_out.fold()

    factor = LOG2E / math.sqrt(DH)
    scale = 1.0 / math.sqrt(DH)

    def head(i, h):
        lanes = at(h, DH)
        here = pl.ds(i * BLOCK, BLOCK)
        seen = pl.ds(i * BLOCK, span)
        part_query = query[here, lanes]
        part_grad = att_grad[lanes, here]
        scores = against(window[seen, 0:DH], part_query) * factor + bias[i]
        probs = jnp.exp2(scores - lse[h * B + i][0:1])
        grad_probs = product(window[seen, DH:], part_grad)
        centre = jnp.sum(
            att[lanes, here].astype(F32) * part_grad.astype(F32), axis=0, keepdims=True
        )
        grad_scores = (probs * (grad_probs - centre)).astype(BF)
        kv_sum[seen, DH:] += against(probs.astype(BF), part_grad)
        kv_sum[seen, 0:DH] += product(grad_scores, part_query)
        query_grad_t[lanes, here] = (product(keys_t[:, seen], grad_scores) * scale).astype(BF)

    pieces = [(i, g) for i in range(B) for g in range(4)]
    for n, (i, g) in enumerate(pieces):
        loop(H // 4, lambda k: head(i, g * (H // 4) + k))
        if with_slab and n == 2:
            near_out.second()
        if with_slab and n == 5:
            near_out.third()
        if n in (1, 4, 7):
            advance()

    kv_send[:, 0:DH] = (kv_sum[pl.ds(0, 2 * T), 0:DH] * scale).astype(BF)
    kv_send[:, DH:] = kv_sum[pl.ds(0, 2 * T), DH:].astype(BF)
    returns = []
    for d in (1, 2):
        to = (p.row, lax.rem(p.col - d + 2 * p.Z, 2 * p.Z))
        copy = remote(
            kv_send.at[pl.ds((2 - d) * T, T)], kv_recv.at[d - 1], ksend.at[d - 1], krecv.at[d - 1], to
        )
        pl.when(spot - d >= 0)(copy.start)
        returns.append((d, copy))

    def turn(t):
        query_grad[at(t, BLOCK)] = query_grad_t[:, at(t, BLOCK)].T

    loop(B, turn)

    def query_weight_grad(t):
        put(weight_grads[1], t, slice(0, E), product(attn_in_t[at(t, BLOCK)], query_grad[...]))

    loop(D // BLOCK, query_weight_grad)
    if with_slab:
        near_query = Near(1)

    def input_grad_query(t):
        rows = at(t, 128)
        grad_tokens[rows] = against(query_grad[rows], slabs[:, 0:E])

    loop(T // 128, input_grad_query)
    kv_grad[:, 0:DH] = kv_sum[pl.ds(2 * T, T), 0:DH] * scale
    kv_grad[:, DH:] = kv_sum[pl.ds(2 * T, T), DH:]
    if with_slab:
        near_query.fold()
    for d, copy in returns:
        @pl.when(spot + d < pack.size)
        def _():
            copy.wait_recv()
            kv_grad[...] += kv_recv[d - 1].astype(F32)

    window[pl.ds(0, T)] = kv_grad[...].astype(BF)

    def keyval_weight_grad(t):
        put(weight_grads[2], t, slice(0, 2 * DH), product(attn_in_t[at(t, BLOCK)], window[pl.ds(0, T)]))

    loop(D // BLOCK, keyval_weight_grad)

    def input_grad(t, total):
        rows = at(t, 128)
        grad = grad_tokens[rows] + against(window[rows], slabs[:, E:QK])
        value = tokens[rows].astype(F32)
        scale_first = rms_scale(value)
        total = total + fold_rows(grad * (value * scale_first))
        m = grad * gains[0:1]
        grad_tokens[rows] = grad_in[rows] + scale_first * m - value * (
            scale_first * scale_first * scale_first * jnp.mean(m * value, axis=-1, keepdims=True)
        )
        return total

    total = lax.fori_loop(0, T // 128, input_grad, jnp.zeros((8, D), F32))
    gain_rows[0:1] = jnp.sum(total, axis=0, keepdims=True)

    def gain_grad(t):
        put(weight_grads[2], t, slice(2 * DH, 2 * DH + 128), gain_rows[:, at(t, BLOCK)].T)

    loop(D // BLOCK, gain_grad)
    if with_slab:
        near_rest = Near(2)
        near_query.second()
        near_rest.fold()
        near_query.third()
        near_rest.second()
        near_out.last(out_slab)
        near_rest.third()
    else:
        for ref, out in zip(weight_grads, (out_slab, query_slab, rest_slab)):
            out[...] = ref[...]
    out_copy.wait_recv()

    def join(t):
        rows = at(t, 64)
        output[rows] = (out_own[rows] + out_pair[rows].astype(F32)).astype(BF)

    loop(T // 64, join)
    while ticks:
        advance()
    if with_slab:
        near_query.last(query_slab)
        near_rest.last(rest_slab)
    out_copy.wait_send()
    for d, copy in returns:
        pl.when(spot - d >= 0)(copy.wait_send)
    far.finish()


def backward(
    shape, with_slab, tokens, cot, grad_in, middle, out_own, out_far, slabs, query, window, bias, att, lse, grads
):
    X, Y, Z = sides(shape)
    R = shape[0]
    T, D = tokens.shape
    E, hz = H * DH, grads.shape[2] // 3
    W = slabs.shape[1]
    B = T // BLOCK
    span = WINDOW + BLOCK
    K = Z // 2
    near, far = scatter_count(X, Y, Z), scatter_count(X, Y, K)
    S, V = jax.ShapeDtypeStruct, pltpu.VMEM
    block = (D // R, 3 * hz)
    half = (block[0] // 2, block[1])
    widths = (E, E, 2 * DH + 128)
    ar = D // (R * Z * 2)
    if with_slab:
        slab_outs = [S((ar, w), F32) for w in widths]
        slab_work = [V((R * Z, 2, ar, w), BF) for w in widths]
    else:
        slab_outs = [S((D, w), BF) for w in widths]
        slab_work = [V((D, w), BF) for w in widths]
    outs = [S((T, D), BF), S((T, D), F32), S(block, F32)] + slab_outs
    scratch = [
        V((T, D), BF), V((T, D), BF), V((T, D), F32), V((T, D), F32), V((D, W), BF), V((T, E), BF),
        V((3 * T, 2 * DH), BF), V((B, span, BLOCK), F32), V((E, T), BF), V((H * B, 8, BLOCK), F32),
        V((T, D), F32), V((T, D), BF),
        V((8, D), F32), V((DH, 3 * T), BF), V((T, D), BF), V((E, T), BF), V((E, T), BF), V((T, E), BF),
        V((3 * T, 2 * DH), F32), V((2 * T, 2 * DH), BF), V((2, T, 2 * DH), BF), V((T, 2 * DH), F32),
        V((D, T), BF), V((128, D), F32),
        V((K, X - 1) + half, BF), V((K, Y - 1) + half, BF), V((K,) + block, BF),
        *slab_work,
        *scatter_scratch(X, Y, K, block),
    ]
    if with_slab:
        scratch += [V((R * Z, ar, w), BF) for w in widths]
        for w in widths:
            scratch += scatter_scratch(X, Y, Z, (ar, w))
    scratch += [
        DMA((far,)), DMA((far,)), DMA((3,)), DMA((3,)), DMA((11,)), DMA((K * (X + Y - 1),)),
    ]
    if with_slab:
        scratch += [DMA((near,))] * 6 + [DMA((3,))] * 2
    return pl.pallas_call(
        functools.partial(backward_kernel, shape, with_slab, (D, T, W, hz)),
        out_shape=outs,
        in_specs=[ANY] * 13,
        out_specs=[VM] * 6,
        scratch_shapes=scratch,
        compiler_params=pltpu.CompilerParams(
            collective_id=1, has_side_effects=True, vmem_limit_bytes=62 << 20
        ),
        name="backward",
    )(tokens, cot, grad_in, middle, out_own, out_far, slabs, query, window, bias, att, lse, grads)


def shards(
    shape,
    tokens, gain_attn, w_query, w_keyval, w_out, gain_mlp, w_gate, w_up, w_down, segment, cotangent
):
    with_slab = w_query.shape[0] % 32 == 0
    ffn = jnp.concatenate([w_gate, w_up, w_down.T], axis=1)
    gain_columns = jnp.pad(jnp.stack([gain_attn, gain_mlp], axis=1), ((0, 0), (0, 126)))
    slab = jnp.concatenate([w_query, w_keyval, gain_columns, w_out], axis=1)
    if not with_slab:
        slab = lax.all_gather(slab, ("row", "col"), axis=0, tiled=True)
    marks = jnp.broadcast_to(segment.astype(F32)[None], (8, segment.shape[0]))
    kept = forward(shape, with_slab, tokens, cotangent, marks, slab, ffn)
    output, grad_tokens, ffn_grad, *slab_grads = backward(shape, with_slab, tokens, cotangent, *kept)
    if not with_slab:
        slab_grads = [
            lax.psum_scatter(g.astype(F32), ("row", "col"), scatter_dimension=0, tiled=True)
            for g in slab_grads
        ]
    out_grad, query_grad, rest_grad = slab_grads
    hz = w_gate.shape[1]
    return (
        output,
        grad_tokens,
        rest_grad[:, 2 * DH],
        query_grad,
        rest_grad[:, : 2 * DH],
        out_grad,
        rest_grad[:, 2 * DH + 1],
        ffn_grad[:, :hz],
        ffn_grad[:, hz : 2 * hz],
        ffn_grad[:, 2 * hz :].T,
    )


def solution(mesh):
    shape = (mesh.shape["row"], mesh.shape["col"])
    return jax.shard_map(
        functools.partial(shards, shape),
        mesh=mesh,
        in_specs=(
            P(("row", "col"), None),
            P(("row", "col")),
            P(("row", "col"), None),
            P(("row", "col"), None),
            P(("row", "col"), None),
            P(("row", "col")),
            P("row", "col"),
            P("row", "col"),
            P("col", "row"),
            P(("row", "col")),
            P(("row", "col"), None),
        ),
        out_specs=(
            P(("row", "col"), None),
            P(("row", "col"), None),
            P(("row", "col")),
            P(("row", "col"), None),
            P(("row", "col"), None),
            P(("row", "col"), None),
            P(("row", "col")),
            P("row", "col"),
            P("row", "col"),
            P("col", "row"),
        ),
        check_vma=False,
    )
```

time: 322 us -> 261 us (0.81)
  Pallas kernels: 304 us -> 243 us
    pallas_call x1, Pallas kernels: 153 us -> 99.7 us  [backward(): pl.pallas_call(functools.partial(backward_kernel, shape, with_slab, (D, T...]
    pallas_call x1, Pallas kernels: 151 us -> 143 us  [forward(): pl.pallas_call(functools.partial(forward_kernel, shape, with_slab, (D, T,...]
where the time goes in v1:
time: 261 us; the launch traced here: 260 us
  Pallas kernels  243 us (93%)
  local copies, waits for them, and re-layouts  11.6 us (4%)
  other arithmetic  4.82 us (2%)
    pallas_call x1, Pallas kernels, forward(): pl.pallas_call(functools.partial(forward_kernel, shape, with_slab, (D, T,...  143 us
    pallas_call x1, Pallas kernels, backward(): pl.pallas_call(functools.partial(backward_kernel, shape, with_slab, (D, T...  99.7 us
    unnamed x14, local copies, waits for them, and re-layouts  5.62 us

profile of v1, /device:TPU:0, one launch (start us, length us, event | category | flops | bytes accessed | tf_op | source)
XLA Modules:
  0.0 260.2 jit_solution(17334528147415654115)
XLA Ops:
  0.6 0.7 pad_maximum_fusion.1
  1.3 0.7 convert_element_type.5
  2.0 0.1 copy.29
  2.1 0.6 broadcast_in_dim.2.refs_2_
  2.7 1.6 fusion.3.refs_3_
  4.3 1.1 copy.30
  5.4 1.9 pad_maximum_fusion.refs_4_
  7.3 143.5 %forward.1 = (f32[512,1024]{1,0:T(8,128)}, f32[512,1024]{1,0:T(8,128)}, f32[512,1024]{1,0:T(8,128)}, bf16[512,1024]{1,0:T(8,128)(2,1)}, bf16[1024,2432]{1,0:T(8,...) custom-call(bf16[512,1024]{1,0:T(8,128)(2,1)} %refs_0_.3, ...), custom_call_target="tpu_custom_call" | custom-call | tf_op jit(solution)/shard_map/forward/pallas_call | solution.py:705
  150.7 99.7 %backward.1 = (bf16[512,1024]{1,0:T(8,128)(2,1)}, f32[512,1024]{1,0:T(8,128)}, f32[256,1152]{1,0:T(8,128)}, f32[32,1024]{1,0:T(8,128)}, f32[32,1024]{1,0:T(8,128)}, /*index=5*/f32[32,384]{1,0:T(8,128)}) custom-call(bf16[512,1024]{1,0:T(8,128)(2,1)} %refs_0_.3, bf16[512,1024]{1,0:T(8,128)(2,1)} %refs_1_.3, f32[512,1024]{1,0:T(8,128)} %get-tuple-element.27.refs_2_, ...), custom_call_target="tpu_custom_call" | custom-call | tf_op jit(solution)/shard_map/backward/pallas_call | solution.py:1090
  250.4 0.0 copy-start.1
  250.4 1.5 slice_reduce_fusion
  251.9 1.4 slice.19
  253.3 0.0 copy-start
  253.3 2.3 slice_bitcast_fusion
  255.7 0.9 copy.31
  256.6 0.0 copy-done.1
  256.6 1.0 copy.36
  257.5 0.0 copy-done
  257.5 0.0 copy-start.3
  257.5 1.3 copy.37
  258.9 0.0 copy-done.3
  258.9 0.7 copy.38
  259.5 0.0 copy-done.2
  259.5 0.7 copy.39
  (1 shorter events, 0.0 us)
Async XLA Ops:
  250.4 6.2 %copy-start.1 = (bf16[512,1024]{1,0:T(8,128)(2,1)S(1)}, bf16[512,1024]{1,0:T(8,128)(2,1)}, u32[]{:S(2)}) copy-start(bf16[512,1024]{1,0:T(8,128)(2,1)} %get-tuple-element.89) | copy-start | bytes 3145732
  253.3 4.2 %copy-start = (f32[512,1024]{1,0:T(8,128)S(1)}, f32[512,1024]{1,0:T(8,128)}, u32[]{:S(2)}) copy-start(f32[512,1024]{1,0:T(8,128)} %get-tuple-element.90) | copy-start | bytes 6291460
  257.5 1.3 copy-start.3
  257.5 2.0 copy-start.2

commit v2 on v1

--- a/solution.py
+++ b/solution.py
@@ -326,13 +326,13 @@
 
 def forward_kernel(shape, with_slab, sizes, *refs):
     D, T, W, hz = sizes
-    (tokens, cot, marks, slab, ffn,
-     grad_in, middle, out_own, out_far, slabs_out, query_out, window_out, bias_out, att_out, lse_out, grads_out,
+    (tokens, cot, segment, w_gate, w_up, w_down, *slab_in) = refs[: 10 if with_slab else 7]
+    (grad_in, middle, out_own, out_far, slabs_out, query_out, window_out, bias_out, att_out, lse_out, grads_out,
      slabs, ffns, query, window, values_t, marks_all, bias, att, lse, gains, mlp, cots,
      grad_tile, out_tile, hidden, grad_act, side_grad, side_out, cross_grad, cross_out, far_grad,
      mate_grad, mate_out, pre_grad, pre_out, pair_grad,
-     asend, arecv, osend, orecv, fsend, frecv, csend, crecv, ksend, krecv, tsend, trecv, msend, mrecv,
-     gsend, grecv, lsem, gsem) = refs
+     vsend, vrecv, asend, arecv, osend, orecv, fsend, frecv, csend, crecv, ksend, krecv, tsend, trecv,
+     msend, mrecv, gsend, grecv, lsem, gsem) = refs[10 if with_slab else 7 :]
     p = Place(shape)
     pack = Pack(p, T)
     mate, pair, spot = pack.mate, pack.pair, pack.spot
@@ -349,20 +349,28 @@
     ready = pack.greet()
     load_cot = local(cot, cots.at[pl.ds(0, T)], 0)
     if not with_slab:
-        load_slab = local(slab, slabs, 1)
-    ready()
-
-    br = ffn.shape[0]
+        load_slab = local(slab_in[0], slabs, 1)
+    br = w_gate.shape[0]
+    own_rows = at(p.row, br)
+    ffns[0, own_rows, 0:hz] = w_gate[...]
+    ffns[0, own_rows, hz : 2 * hz] = w_up[...]
+    ffns[0, own_rows, 2 * hz :] = w_down[...].T
 
     def ffn_at(s, r, half):
         if half is None:
             return ffns.at[s, at(r, br)]
         return ffns.at[s, pl.ds(pl.multiple_of(r * br + half * (br // 2), br // 2), br // 2)]
 
-    far = Gather(ffn_at, lambda k: ffn_at(k, p.row, None), p, Sems(fsend, frecv), ffn, 2)
-
-    if with_slab:
-        ar = slab.shape[0]
+    far = Gather(
+        ffn_at, lambda k: ffn_at(k, p.row, None), p, Sems(fsend, frecv), ffn_at(0, p.row, None), 2
+    )
+
+    if with_slab:
+        ar = slab_in[0].shape[0]
+        slab_rows = pl.ds(pl.multiple_of(((p.row * p.Z + p.z) * 2 + p.core) * ar, ar), ar)
+        widths = ((0, E), (E, QK), (QK, WO), (WO, W))
+        for piece, (start, stop) in zip(slab_in, widths):
+            slabs[slab_rows, start:stop] = piece[...]
 
         def slab_place(lanes, core):
             def place(s, r, half):
@@ -376,9 +384,11 @@
 
         def slab_gather(lanes, sems):
             place = slab_place(lanes, p.core)
-            return Gather(place, lambda k: place(0, p.row, None), p, sems, slab.at[:, lanes])
-
-        act_lanes, out_lanes = slice(0, WO), slice(WO, W)
+            own = place(0, p.row, None)
+            return Gather(place, lambda k: own, p, sems, own)
+
+        rest_lanes, act_lanes, out_lanes = slice(E, WO), slice(0, E), slice(WO, W)
+        near_rest = slab_gather(rest_lanes, Sems(vsend, vrecv))
         near = slab_gather(act_lanes, Sems(asend, arecv))
         near_out = slab_gather(out_lanes, Sems(osend, orecv))
         hands = Sems(csend, crecv)
@@ -398,11 +408,20 @@
                         passed.append((copy, remote(other, other, send, recv, mate)))
             return passed
 
+        def settle(passed):
+            for copy, arrival in passed:
+                copy.wait_send()
+                arrival.wait_recv()
+
+    ready()
+    if with_slab:
+        near_rest.spread_z()
+        near_rest.spread_xy(0)
         near.spread_z()
         near.spread_xy(0)
         near_out.spread_z()
 
-    marks_all[:, pl.ds(2 * T, T)] = marks[...]
+    marks_all[:, pl.ds(2 * T, T)] = jnp.broadcast_to(segment[...].astype(F32), (8, T))
 
     @pl.when(spot == 0)
     def _():
@@ -434,33 +453,26 @@
 
     load_cot.wait()
     cot_mate = remote(whole(cots, 0), whole(cots, 1), tsend.at[0], trecv.at[0], mate)
-    cot_pair = remote(whole(cots, 0), whole(cots, 2), tsend.at[1], trecv.at[1], pair)
-    cot_pass = remote(whole(cots, 2), whole(cots, 3), tsend.at[2], trecv.at[2], mate)
     cot_mate.start()
-    if with_slab:
-        slabs[pl.ds(pl.multiple_of(((p.row * p.Z + p.z) * 2 + p.core) * ar, ar), ar)] = slab[...]
-    ffns[0, at(p.row, br)] = ffn[...]
+
+    def tile_of(ref, n, i):
+        return ref.at[pl.ds(pl.multiple_of(n * T + i * BLOCK, BLOCK), BLOCK)]
+
+    def cot_copy(n, i):
+        to, src, sem = (pair, 0, 1 + i) if n == 2 else (mate, 2, 1 + B + i)
+        return remote(tile_of(cots, src, i), tile_of(cots, n, i), tsend.at[sem], trecv.at[sem], to)
+
     if with_slab:
         for s in range(p.Z):
-            near.spread_xy(s + 1)
-            if s == 0:
-                near_out.spread_xy(0)
+            near_rest.spread_xy(s + 1)
+            near_rest.spread_diagonal(s)
+        for s in range(1, p.Z):
+            near.spread_xy(s)
+        passed = hand(near_rest, rest_lanes)
+        for s in range(p.Z):
             near.spread_diagonal(s)
-        far.spread_z()
-        cot_pair.start()
-        for s in range(1, p.Z):
-            near_out.spread_xy(s)
-        passed = hand(near, act_lanes)
-        far.spread_xy(0)
-        for s in range(p.Z):
-            near_out.spread_diagonal(s)
-        for copy, arrival in passed:
-            copy.wait_send()
-            arrival.wait_recv()
+        settle(passed)
     else:
-        far.spread_z()
-        cot_pair.start()
-        far.spread_xy(0)
         load_slab.wait()
     gains[...] = slabs[:, QK:WO].astype(F32).T[0:8]
 
@@ -474,13 +486,22 @@
     key_place = lambda k: window.at[pl.ds(k * T, T)]
     behind(key_place(2), key_place, 3, "start")
 
+    far.spread_z()
+    cot_copy(2, 0).start()
+    if with_slab:
+        for s in range(p.Z):
+            near_out.spread_xy(s)
+        settle(hand(near, act_lanes))
+
     def project(t):
         query[at(t, BLOCK)] = product(mlp[at(t, BLOCK)], slabs[:, 0:E]).astype(BF)
 
     loop(B, project)
     save_query = local(query, query_out, 2)
     if with_slab:
-        passed = hand(near_out, out_lanes)
+        for s in range(p.Z):
+            near_out.spread_diagonal(s)
+    far.spread_xy(0)
     behind(mark_own, mark_place, 0, "arrive")
     column = jnp.broadcast_to(marks_all[0:1], (128, 3 * T)).T
     for i in range(B):
@@ -494,7 +515,11 @@
         allowed = (keys_at == own) & (gap >= 0) & (gap < WINDOW)
         bias[i] = jnp.where(allowed, 0.0, NEGATIVE)
     save_bias = local(bias, bias_out, 3)
+    if with_slab:
+        passed = hand(near_out, out_lanes)
     behind(key_place(2), key_place, 3, "arrive")
+    for i in range(1, B):
+        cot_copy(2, i).start()
     save_window = local(window, window_out, 4)
     values_t[...] = window[:, DH:].T
     factor = LOG2E / math.sqrt(DH)
@@ -510,9 +535,6 @@
         att[lanes, pl.ds(i * BLOCK, BLOCK)] = (mixed / total).astype(BF)
         lse[h * B + i] = jnp.broadcast_to(top + jnp.log2(total), (8, BLOCK))
 
-    def tile_of(ref, n, i):
-        return ref.at[pl.ds(pl.multiple_of(n * T + i * BLOCK, BLOCK), BLOCK)]
-
     def mlp_copy(n, i):
         to = pair if n == 2 else mate
         src = 2 if n == 3 else 0
@@ -526,9 +548,7 @@
             far.spread_diagonal(0)
             loop(H // 2, lambda h: head(i, h + H // 2))
             if with_slab:
-                for copy, arrival in passed:
-                    copy.wait_send()
-                    arrival.wait_recv()
+                settle(passed)
             save_slabs = local(slabs, slabs_out, 1)
         else:
             loop(H, lambda h: head(i, h))
@@ -543,9 +563,8 @@
         loop(BLOCK // 64, second_norm)
         mlp_copy(1, i).start()
         mlp_copy(2, i).start()
-        if i == 0:
-            cot_pair.wait_recv()
-            cot_pass.start()
+        cot_copy(2, i).wait_recv()
+        cot_copy(3, i).start()
     save_att = local(att, att_out, 5)
     save_lse = local(lse, lse_out, 6)
     for s in range(2, K):
@@ -557,7 +576,8 @@
     for s in range(K):
         far.close(s)
     cot_mate.wait()
-    cot_pass.wait_recv()
+    for i in range(B):
+        cot_copy(3, i).wait_recv()
 
     def grad_copy(i):
         return [
@@ -670,19 +690,20 @@
         save.wait()
     behind(mark_own, mark_place, 0, "sent")
     behind(key_place(2), key_place, 3, "sent")
-    cot_pair.wait_send()
-    cot_pass.wait_send()
-    if with_slab:
-        near.finish()
-        near_out.finish()
-
-
-def forward(shape, with_slab, tokens, cot, marks, slab, ffn):
+    for i in range(B):
+        cot_copy(2, i).wait_send()
+        cot_copy(3, i).wait_send()
+    if with_slab:
+        for gather in (near_rest, near, near_out):
+            gather.finish()
+
+
+def forward(shape, with_slab, tokens, cot, segment, w_gate, w_up, w_down, *slab):
     X, Y, Z = sides(shape)
     R = shape[0]
     T, D = tokens.shape
-    E, hz = H * DH, ffn.shape[1] // 3
-    W = slab.shape[1]
+    E, hz = H * DH, w_gate.shape[1]
+    W = 2 * E + 2 * DH + 128
     B = T // BLOCK
     span = WINDOW + BLOCK
     K = Z // 2
@@ -699,20 +720,20 @@
         V((H * B, 8, BLOCK), F32), V((8, D), F32), V((4 * T, D), BF), V((4 * T, D), BF),
         V((BLOCK, D), F32), V((BLOCK, D), F32), V((K, 4 * T, hz), BF), V((K, 4 * T, 2 * hz), BF),
         *[V((T, D), BF)] * 10,
-        *[DMA((near,))] * 4, *[DMA((far,))] * 2, *[DMA((2 * R * Z,))] * 2, *[DMA((6,))] * 2,
-        *[DMA((3,))] * 2, *[DMA((3 * B,))] * 2, *[DMA((5 * B,))] * 2, DMA((7,)), DMA((1,)),
+        *[DMA((near,))] * 6, *[DMA((far,))] * 2, *[DMA((3 * R * Z,))] * 2, *[DMA((6,))] * 2,
+        *[DMA((1 + 2 * B,))] * 2, *[DMA((3 * B,))] * 2, *[DMA((5 * B,))] * 2, DMA((7,)), DMA((1,)),
     ]
     return pl.pallas_call(
         functools.partial(forward_kernel, shape, with_slab, (D, T, W, hz)),
         out_shape=outs,
-        in_specs=[VM, ANY, VM, VM if with_slab else ANY, VM],
+        in_specs=[VM, ANY] + [VM] * 4 + [VM if with_slab else ANY] * len(slab),
         out_specs=[VM] * 4 + [ANY] * 7,
         scratch_shapes=scratch,
         compiler_params=pltpu.CompilerParams(
             collective_id=0, has_side_effects=True, vmem_limit_bytes=62 << 20
         ),
         name="forward",
-    )(tokens, cot, marks, slab, ffn)
+    )(tokens, cot, segment, w_gate, w_up, w_down, *slab)
 
 
 def backward_kernel(shape, with_slab, sizes, *refs):
@@ -729,14 +750,15 @@
 
     (tokens_in, cot_in, grad_in_in, middle_in, out_own_in, out_far,
      slabs_in, query_in, window_in, bias_in, att_in, lse_in, grads) = some(13)
-    output, grad_tokens, ffn_out, out_slab, query_slab, rest_slab = some(6)
+    output, grad_tokens, gate_out, up_out, down_out, out_slab, query_slab = some(7)
+    keyval_slab, gain_slab = some(2) if with_slab else (some(1)[0], None)
     (tokens, cot, middle, grad_in, slabs, query, window, bias, att, lse, out_own, out_pair,
      gains, keys_t, branch, att_grad, query_grad_t, query_grad, kv_sum, kv_send, kv_recv, kv_grad, attn_in_t,
-     gain_rows, termx, termy, own) = some(27)
+     gain_rows, termx, termy, own, ffn_sum) = some(28)
     weight_grads = some(3)
     fwork = some(4)
     if with_slab:
-        crossed = some(3)
+        rest_sum, *crossed = some(4)
         works = [some(4) for _ in range(3)]
     fsend, frecv, ksend, krecv, lsem, tsem = some(6)
     if with_slab:
@@ -807,7 +829,7 @@
                         copy.wait()
                     far.second(s)
                 else:
-                    far.third(s, ffn_out)
+                    far.third(s, ffn_sum)
 
     for s in order[:2]:
         far.first(s)
@@ -940,15 +962,8 @@
         kv_sum[seen, 0:DH] += product(grad_scores, part_query)
         query_grad_t[lanes, here] = (product(keys_t[:, seen], grad_scores) * scale).astype(BF)
 
-    pieces = [(i, g) for i in range(B) for g in range(4)]
-    for n, (i, g) in enumerate(pieces):
-        loop(H // 4, lambda k: head(i, g * (H // 4) + k))
-        if with_slab and n == 2:
-            near_out.second()
-        if with_slab and n == 5:
-            near_out.third()
-        if n in (1, 4, 7):
-            advance()
+    for i in range(B):
+        loop(H, lambda h: head(i, h))
 
     kv_send[:, 0:DH] = (kv_sum[pl.ds(0, 2 * T), 0:DH] * scale).astype(BF)
     kv_send[:, DH:] = kv_sum[pl.ds(0, 2 * T), DH:].astype(BF)
@@ -972,6 +987,7 @@
     loop(D // BLOCK, query_weight_grad)
     if with_slab:
         near_query = Near(1)
+    advance()
 
     def input_grad_query(t):
         rows = at(t, 128)
@@ -982,6 +998,7 @@
     kv_grad[:, DH:] = kv_sum[pl.ds(2 * T, T), DH:]
     if with_slab:
         near_query.fold()
+        near_out.second()
     for d, copy in returns:
         @pl.when(spot + d < pack.size)
         def _():
@@ -1018,12 +1035,14 @@
         near_rest = Near(2)
         near_query.second()
         near_rest.fold()
+        advance()
+        near_out.third()
         near_query.third()
         near_rest.second()
+        near_rest.third()
         near_out.last(out_slab)
-        near_rest.third()
     else:
-        for ref, out in zip(weight_grads, (out_slab, query_slab, rest_slab)):
+        for ref, out in zip(weight_grads, (out_slab, query_slab, keyval_slab)):
             out[...] = ref[...]
     out_copy.wait_recv()
 
@@ -1034,9 +1053,14 @@
     loop(T // 64, join)
     while ticks:
         advance()
+    gate_out[...] = ffn_sum[:, 0:hz]
+    up_out[...] = ffn_sum[:, hz : 2 * hz]
+    down_out[...] = ffn_sum[:, 2 * hz :].T
     if with_slab:
         near_query.last(query_slab)
-        near_rest.last(rest_slab)
+        near_rest.last(rest_sum)
+        keyval_slab[...] = rest_sum[:, 0 : 2 * DH]
+        gain_slab[...] = rest_sum[:, 2 * DH :]
     out_copy.wait_send()
     for d, copy in returns:
         pl.when(spot - d >= 0)(copy.wait_send)
@@ -1061,12 +1085,13 @@
     widths = (E, E, 2 * DH + 128)
     ar = D // (R * Z * 2)
     if with_slab:
-        slab_outs = [S((ar, w), F32) for w in widths]
+        slab_outs = [S((ar, w), F32) for w in (E, E, 2 * DH, 128)]
         slab_work = [V((R * Z, 2, ar, w), BF) for w in widths]
     else:
         slab_outs = [S((D, w), BF) for w in widths]
         slab_work = [V((D, w), BF) for w in widths]
-    outs = [S((T, D), BF), S((T, D), F32), S(block, F32)] + slab_outs
+    outs = [S((T, D), BF), S((T, D), F32)]
+    outs += [S((D // R, hz), F32), S((D // R, hz), F32), S((hz, D // R), F32)] + slab_outs
     scratch = [
         V((T, D), BF), V((T, D), BF), V((T, D), F32), V((T, D), F32), V((D, W), BF), V((T, E), BF),
         V((3 * T, 2 * DH), BF), V((B, span, BLOCK), F32), V((E, T), BF), V((H * B, 8, BLOCK), F32),
@@ -1074,12 +1099,12 @@
         V((8, D), F32), V((DH, 3 * T), BF), V((T, D), BF), V((E, T), BF), V((E, T), BF), V((T, E), BF),
         V((3 * T, 2 * DH), F32), V((2 * T, 2 * DH), BF), V((2, T, 2 * DH), BF), V((T, 2 * DH), F32),
         V((D, T), BF), V((128, D), F32),
-        V((K, X - 1) + half, BF), V((K, Y - 1) + half, BF), V((K,) + block, BF),
+        V((K, X - 1) + half, BF), V((K, Y - 1) + half, BF), V((K,) + block, BF), V(block, F32),
         *slab_work,
         *scatter_scratch(X, Y, K, block),
     ]
     if with_slab:
-        scratch += [V((R * Z, ar, w), BF) for w in widths]
+        scratch += [V((ar, widths[2]), F32)] + [V((R * Z, ar, w), BF) for w in widths]
         for w in widths:
             scratch += scatter_scratch(X, Y, Z, (ar, w))
     scratch += [
@@ -1091,7 +1116,7 @@
         functools.partial(backward_kernel, shape, with_slab, (D, T, W, hz)),
         out_shape=outs,
         in_specs=[ANY] * 13,
-        out_specs=[VM] * 6,
+        out_specs=[VM] * len(outs),
         scratch_shapes=scratch,
         compiler_params=pltpu.CompilerParams(
             collective_id=1, has_side_effects=True, vmem_limit_bytes=62 << 20
@@ -1105,32 +1130,32 @@
     tokens, gain_attn, w_query, w_keyval, w_out, gain_mlp, w_gate, w_up, w_down, segment, cotangent
 ):
     with_slab = w_query.shape[0] % 32 == 0
-    ffn = jnp.concatenate([w_gate, w_up, w_down.T], axis=1)
     gain_columns = jnp.pad(jnp.stack([gain_attn, gain_mlp], axis=1), ((0, 0), (0, 126)))
-    slab = jnp.concatenate([w_query, w_keyval, gain_columns, w_out], axis=1)
+    slab = [w_query, w_keyval, gain_columns, w_out]
     if not with_slab:
-        slab = lax.all_gather(slab, ("row", "col"), axis=0, tiled=True)
-    marks = jnp.broadcast_to(segment.astype(F32)[None], (8, segment.shape[0]))
-    kept = forward(shape, with_slab, tokens, cotangent, marks, slab, ffn)
-    output, grad_tokens, ffn_grad, *slab_grads = backward(shape, with_slab, tokens, cotangent, *kept)
-    if not with_slab:
-        slab_grads = [
+        slab = [lax.all_gather(jnp.concatenate(slab, axis=1), ("row", "col"), axis=0, tiled=True)]
+    kept = forward(shape, with_slab, tokens, cotangent, segment[None], w_gate, w_up, w_down, *slab)
+    results = backward(shape, with_slab, tokens, cotangent, *kept)
+    output, grad_tokens, gate_grad, up_grad, down_grad = results[:5]
+    if with_slab:
+        out_grad, query_grad, keyval_grad, gain_grad = results[5:]
+    else:
+        out_grad, query_grad, rest_grad = [
             lax.psum_scatter(g.astype(F32), ("row", "col"), scatter_dimension=0, tiled=True)
-            for g in slab_grads
+            for g in results[5:]
         ]
-    out_grad, query_grad, rest_grad = slab_grads
-    hz = w_gate.shape[1]
+        keyval_grad, gain_grad = rest_grad[:, : 2 * DH], rest_grad[:, 2 * DH :]
     return (
         output,
         grad_tokens,
-        rest_grad[:, 2 * DH],
+        gain_grad[:, 0],
         query_grad,
-        rest_grad[:, : 2 * DH],
+        keyval_grad,
         out_grad,
-        rest_grad[:, 2 * DH + 1],
-        ffn_grad[:, :hz],
-        ffn_grad[:, hz : 2 * hz],
-        ffn_grad[:, 2 * hz :].T,
+        gain_grad[:, 1],
+        gate_grad,
+        up_grad,
+        down_grad,
     )
 
 

time: 261 us -> 229 us (0.88)
  Pallas kernels: 243 us -> 218 us
  other arithmetic: 4.82 us -> 0.68 us
    pallas_call x1, Pallas kernels: 143 us -> 124 us  [forward(): pl.pallas_call(functools.partial(forward_kernel, shape, with_slab, (D, T,...]
    pallas_call x1, Pallas kernels: 99.7 us -> 93.4 us  [backward(): pl.pallas_call(functools.partial(backward_kernel, shape, with_slab, (D, T...]
    concatenate x2 -> x0, other arithmetic: 3.45 us -> none  [the longest x1 1.89 us: shards(): ffn = jnp.concatenate([w_gate, w_up, w_down.T], axis=1)]
    unnamed x14 -> x22, local copies, waits for them, and re-layouts: 5.62 us -> 7.77 us
where the time goes in v2:
time: 229 us
  Pallas kernels  218 us (95%)
  local copies, waits for them, and re-layouts  10.1 us (4%)
    pallas_call x1, Pallas kernels, forward(): pl.pallas_call(functools.partial(forward_kernel, shape, with_slab, (D, T,...  124 us
    pallas_call x1, Pallas kernels, backward(): pl.pallas_call(functools.partial(backward_kernel, shape, with_slab, (D, T...  93.4 us
    unnamed x22, local copies, waits for them, and re-layouts  7.77 us

profile of v2, /device:TPU:0, one launch (start us, length us, event | category | flops | bytes accessed | tf_op | source)
XLA Modules:
  0.0 229.0 jit_solution(5564052354842412773)
XLA Ops:
  0.6 0.7 pad_maximum_fusion
  1.3 0.1 copy.25
  1.4 0.6 pad.4.refs_8_
  2.0 124.2 %forward.1 = (f32[512,1024]{1,0:T(8,128)}, f32[512,1024]{1,0:T(8,128)}, f32[512,1024]{1,0:T(8,128)}, bf16[512,1024]{1,0:T(8,128)(2,1)}, bf16[1024,2432]{1,0:T(8,...) custom-call(bf16[512,1024]{1,0:T(8,128)(2,1)} %refs_0_.3, ...), custom_call_target="tpu_custom_call" | custom-call | tf_op jit(solution)/shard_map/forward/pallas_call | solution.py:726
  126.2 93.4 %backward.1 = (bf16[512,1024]{1,0:T(8,128)(2,1)}, f32[512,1024]{1,0:T(8,128)}, f32[256,384]{1,0:T(8,128)}, f32[256,384]{1,0:T(8,128)}, f32[384,256]{1,0:T(8,128)...) custom-call(bf16[512,1024]{1,0:T(8,128)(2,1)} %refs_0_.3, ...), custom_call_target="tpu_custom_call" | custom-call | tf_op jit(solution)/shard_map/backward/pallas_call | solution.py:1115
  219.6 0.0 copy-start
  219.7 1.6 slice_reduce_fusion
  221.2 2.3 copy.34
  223.5 0.0 copy-done
  223.5 0.0 copy-start.3
  223.5 0.0 copy-start.2
  223.5 1.3 copy.35
  224.8 0.0 copy-done.5
  224.9 0.7 copy.36
  225.5 0.0 copy-done.6
  225.5 0.6 copy.37
  226.1 0.0 copy-done.4
  226.1 0.7 copy.38
  226.8 0.0 copy-done.3
  226.8 0.7 copy.39
  227.5 0.0 copy-done.2
  227.5 0.7 copy.40
  228.3 0.0 copy-done.1
  228.3 0.7 copy.41
  (4 shorter events, 0.0 us)
Async XLA Ops:
  219.6 3.9 %copy-start = (f32[512,1024]{1,0:T(8,128)S(1)}, f32[512,1024]{1,0:T(8,128)}, u32[]{:S(2)}) copy-start(f32[512,1024]{1,0:T(8,128)} %get-tuple-element.63) | copy-start | bytes 6291460
  223.5 1.4 copy-start.5
  223.5 2.0 copy-start.6
  223.5 2.6 %copy-start.4 = (f32[32,1024]{1,0:T(8,128)S(1)}, f32[32,1024]{1,0:T(8,128)}, u32[]{:S(2)}) copy-start(f32[32,1024]{1,0:T(8,128)} %get-tuple-element.67) | copy-start | bytes 393220
  223.5 3.3 %copy-start.3 = (f32[256,384]{1,0:T(8,128)S(1)}, f32[256,384]{1,0:T(8,128)}, u32[]{:S(2)}) copy-start(f32[256,384]{1,0:T(8,128)} %get-tuple-element.69) | copy-start | bytes 1179652
  223.5 4.0 %copy-start.2 = (f32[256,384]{1,0:T(8,128)S(1)}, f32[256,384]{1,0:T(8,128)}, u32[]{:S(2)}) copy-start(f32[256,384]{1,0:T(8,128)} %get-tuple-element.70) | copy-start | bytes 1179652
  224.9 3.4 %copy-start.1 = (f32[384,256]{1,0:T(8,128)S(1)}, f32[384,256]{1,0:T(8,128)}, u32[]{:S(2)}) copy-start(f32[384,256]{1,0:T(8,128)} %get-tuple-element.71) | copy-start | bytes 1179652

commit v3 on v2

--- a/solution.py
+++ b/solution.py
@@ -327,8 +327,8 @@
 def forward_kernel(shape, with_slab, sizes, *refs):
     D, T, W, hz = sizes
     (tokens, cot, segment, w_gate, w_up, w_down, *slab_in) = refs[: 10 if with_slab else 7]
-    (grad_in, middle, out_own, out_far, slabs_out, query_out, window_out, bias_out, att_out, lse_out, grads_out,
-     slabs, ffns, query, window, values_t, marks_all, bias, att, lse, gains, mlp, cots,
+    (grad_in, middle, out_own, out_far, gains, slabs_out, query_out, window_out, bias_out, att_out, lse_out, grads_out,
+     slabs, ffns, query, window, values_t, marks_all, bias, att, lse, mlp, cots,
      grad_tile, out_tile, hidden, grad_act, side_grad, side_out, cross_grad, cross_out, far_grad,
      mate_grad, mate_out, pre_grad, pre_out, pair_grad,
      vsend, vrecv, asend, arecv, osend, orecv, fsend, frecv, csend, crecv, ksend, krecv, tsend, trecv,
@@ -667,10 +667,13 @@
         for s in range(K):
             ffns[s, rows, 0 : 2 * hz] = inner(mlp[:, rows], grad_act[s]).astype(BF)
             ffns[s, rows, 2 * hz :] = inner(cots[:, rows], hidden[s]).astype(BF)
+        save_grads(t).start()
+
+    def save_grads(t):
+        rows = at(t, BLOCK)
+        return pltpu.make_async_copy(ffns.at[:, rows], grads_out.at[:, rows], gsem.at[t])
 
     loop(D // BLOCK, weight_tile)
-    save_grads = pltpu.make_async_copy(ffns, grads_out, gsem.at[0])
-    save_grads.start()
 
     def join(t):
         rows = at(t, 64)
@@ -686,8 +689,10 @@
         for n in (1, 2, 3):
             mlp_copy(n, i).wait_send()
     loop(T // 64, join)
-    for save in (save_slabs, save_query, save_bias, save_window, save_att, save_lse, save_grads):
+    for save in (save_slabs, save_query, save_bias, save_window, save_att, save_lse):
         save.wait()
+    for t in range(D // BLOCK):
+        save_grads(t).wait()
     behind(mark_own, mark_place, 0, "sent")
     behind(key_place(2), key_place, 3, "sent")
     for i in range(B):
@@ -709,7 +714,7 @@
     K = Z // 2
     S, V = jax.ShapeDtypeStruct, pltpu.VMEM
     outs = [
-        S((T, D), F32), S((T, D), F32), S((T, D), F32), S((T, D), BF),
+        S((T, D), F32), S((T, D), F32), S((T, D), F32), S((T, D), BF), S((8, D), F32),
         S((D, W), BF), S((T, E), BF), S((3 * T, 2 * DH), BF), S((B, span, BLOCK), F32),
         S((E, T), BF), S((H * B, 8, BLOCK), F32), S((K, D, 3 * hz), BF),
     ]
@@ -717,17 +722,17 @@
     scratch = [
         V((D, W), BF), V((K, D, 3 * hz), BF), V((T, E), BF), V((3 * T, 2 * DH), BF),
         V((DH, 3 * T), BF), V((8, 3 * T), F32), V((B, span, BLOCK), F32), V((E, T), BF),
-        V((H * B, 8, BLOCK), F32), V((8, D), F32), V((4 * T, D), BF), V((4 * T, D), BF),
+        V((H * B, 8, BLOCK), F32), V((4 * T, D), BF), V((4 * T, D), BF),
         V((BLOCK, D), F32), V((BLOCK, D), F32), V((K, 4 * T, hz), BF), V((K, 4 * T, 2 * hz), BF),
         *[V((T, D), BF)] * 10,
         *[DMA((near,))] * 6, *[DMA((far,))] * 2, *[DMA((3 * R * Z,))] * 2, *[DMA((6,))] * 2,
-        *[DMA((1 + 2 * B,))] * 2, *[DMA((3 * B,))] * 2, *[DMA((5 * B,))] * 2, DMA((7,)), DMA((1,)),
+        *[DMA((1 + 2 * B,))] * 2, *[DMA((3 * B,))] * 2, *[DMA((5 * B,))] * 2, DMA((7,)), DMA((D // BLOCK,)),
     ]
     return pl.pallas_call(
         functools.partial(forward_kernel, shape, with_slab, (D, T, W, hz)),
         out_shape=outs,
         in_specs=[VM, ANY] + [VM] * 4 + [VM if with_slab else ANY] * len(slab),
-        out_specs=[VM] * 4 + [ANY] * 7,
+        out_specs=[VM] * 5 + [ANY] * 7,
         scratch_shapes=scratch,
         compiler_params=pltpu.CompilerParams(
             collective_id=0, has_side_effects=True, vmem_limit_bytes=62 << 20
@@ -749,7 +754,7 @@
         return taken
 
     (tokens_in, cot_in, grad_in_in, middle_in, out_own_in, out_far,
-     slabs_in, query_in, window_in, bias_in, att_in, lse_in, grads) = some(13)
+     gains_in, slabs_in, query_in, window_in, bias_in, att_in, lse_in, grads) = some(14)
     output, grad_tokens, gate_out, up_out, down_out, out_slab, query_slab = some(7)
     keyval_slab, gain_slab = some(2) if with_slab else (some(1)[0], None)
     (tokens, cot, middle, grad_in, slabs, query, window, bias, att, lse, out_own, out_pair,
@@ -792,53 +797,37 @@
             pltpu.make_async_copy(a, b, tsem.at[n + i]) for i, (a, b) in enumerate(copies)
         ]
     pairs = [
-        (middle_in, middle), (grad_in_in, grad_in), (cot_in, cot), (slabs_in, slabs), (att_in, att),
+        (middle_in, middle), (grad_in_in, grad_in), (cot_in, cot), (gains_in, gains), (slabs_in, slabs), (att_in, att),
         (tokens_in, tokens), (window_in, window), (query_in, query), (bias_in, bias), (lse_in, lse),
         (out_own_in, out_own),
     ]
     loads = [pltpu.make_async_copy(a, b, lsem.at[n]) for n, (a, b) in enumerate(pairs)]
-    for load in loads:
+    for load in loads[:4]:
         load.start()
-    for s in order:
-        for copy in terms[s]:
-            copy.start()
     ready()
     far = Scatter(
         part, cut, p, Sems(fsend, frecv),
         lambda s, d: termx.at[s, d - 1], lambda s, e: termy.at[s, e - 1], lambda s: own.at[s],
         *fwork, 2
     )
-    ticks = []
-    for j in range(K + 1):
-        tick = []
-        if j >= 1:
-            tick.append(("third", order[j - 1]))
-        if j < K:
-            tick.append(("second", order[j]))
-        if j + 2 < K:
-            tick.append(("first", order[j + 2]))
-        ticks.append(tick)
-
-    def advance():
-        if ticks:
-            for step, s in ticks.pop(0):
-                if step == "first":
-                    far.first(s)
-                elif step == "second":
-                    for copy in terms[s]:
-                        copy.wait()
-                    far.second(s)
-                else:
-                    far.third(s, ffn_sum)
-
-    for s in order[:2]:
+    def far_second():
+        for s in order:
+            for copy in terms[s]:
+                copy.wait()
+            far.second(s)
+
+    for s in order:
         far.first(s)
     out_copy = remote(out_far, out_pair, ksend.at[2], krecv.at[2], pack.pair)
     out_copy.start()
 
     for load in loads[:4]:
         load.wait()
-    gains[...] = slabs[:, QK:WO].astype(F32).T[0:8]
+    for load in loads[4:]:
+        load.start()
+    for s in order:
+        for copy in terms[s]:
+            copy.start()
     gain_rows[...] = jnp.zeros_like(gain_rows)
 
     def fold_rows(value):
@@ -860,11 +849,13 @@
     total = lax.fori_loop(0, T // 64, second_norm, jnp.zeros((8, D), F32))
     gain_rows[1:2] = jnp.sum(total, axis=0, keepdims=True)
 
+    loads[4].wait()
+
     def attended_grad(t):
         att_grad[at(t, BLOCK)] = against(slabs[at(t, BLOCK), WO:], branch[...]).astype(BF)
 
     loop(E // BLOCK, attended_grad)
-    loads[4].wait()
+    loads[5].wait()
     ar = D // (p.R * p.Z * 2)
     blocks = BLOCK // (2 * ar)
 
@@ -928,7 +919,7 @@
     if with_slab:
         near_out = Near(0)
 
-    for load in loads[5:]:
+    for load in loads[6:]:
         load.wait()
 
     def first_norm(t):
@@ -976,6 +967,10 @@
         pl.when(spot - d >= 0)(copy.start)
         returns.append((d, copy))
 
+    far_second()
+    if with_slab:
+        near_out.second()
+
     def turn(t):
         query_grad[at(t, BLOCK)] = query_grad_t[:, at(t, BLOCK)].T
 
@@ -987,7 +982,6 @@
     loop(D // BLOCK, query_weight_grad)
     if with_slab:
         near_query = Near(1)
-    advance()
 
     def input_grad_query(t):
         rows = at(t, 128)
@@ -998,7 +992,6 @@
     kv_grad[:, DH:] = kv_sum[pl.ds(2 * T, T), DH:]
     if with_slab:
         near_query.fold()
-        near_out.second()
     for d, copy in returns:
         @pl.when(spot + d < pack.size)
         def _():
@@ -1033,9 +1026,11 @@
     loop(D // BLOCK, gain_grad)
     if with_slab:
         near_rest = Near(2)
+    for s in order[:-1]:
+        far.third(s)
+    if with_slab:
         near_query.second()
         near_rest.fold()
-        advance()
         near_out.third()
         near_query.third()
         near_rest.second()
@@ -1051,8 +1046,7 @@
         output[rows] = (out_own[rows] + out_pair[rows].astype(F32)).astype(BF)
 
     loop(T // 64, join)
-    while ticks:
-        advance()
+    far.third(0, ffn_sum)
     gate_out[...] = ffn_sum[:, 0:hz]
     up_out[...] = ffn_sum[:, hz : 2 * hz]
     down_out[...] = ffn_sum[:, 2 * hz :].T
@@ -1068,7 +1062,7 @@
 
 
 def backward(
-    shape, with_slab, tokens, cot, grad_in, middle, out_own, out_far, slabs, query, window, bias, att, lse, grads
+    shape, with_slab, tokens, cot, grad_in, middle, out_own, out_far, gains, slabs, query, window, bias, att, lse, grads
 ):
     X, Y, Z = sides(shape)
     R = shape[0]
@@ -1108,21 +1102,47 @@
         for w in widths:
             scratch += scatter_scratch(X, Y, Z, (ar, w))
     scratch += [
-        DMA((far,)), DMA((far,)), DMA((3,)), DMA((3,)), DMA((11,)), DMA((K * (X + Y - 1),)),
+        DMA((far,)), DMA((far,)), DMA((3,)), DMA((3,)), DMA((12,)), DMA((K * (X + Y - 1),)),
     ]
     if with_slab:
         scratch += [DMA((near,))] * 6 + [DMA((3,))] * 2
     return pl.pallas_call(
         functools.partial(backward_kernel, shape, with_slab, (D, T, W, hz)),
         out_shape=outs,
-        in_specs=[ANY] * 13,
+        in_specs=[ANY] * 14,
         out_specs=[VM] * len(outs),
         scratch_shapes=scratch,
         compiler_params=pltpu.CompilerParams(
             collective_id=1, has_side_effects=True, vmem_limit_bytes=62 << 20
         ),
         name="backward",
-    )(tokens, cot, grad_in, middle, out_own, out_far, slabs, query, window, bias, att, lse, grads)
+    )(tokens, cot, grad_in, middle, out_own, out_far, gains, slabs, query, window, bias, att, lse, grads)
+
+
+def hand_over_kernel(count, *refs):
+    sources, results, held, sems = refs[:count], refs[count : 2 * count], refs[2 * count : -1], refs[-1]
+    reads = [pltpu.make_async_copy(a, b, sems.at[0, n]) for n, (a, b) in enumerate(zip(sources, held))]
+    writes = [pltpu.make_async_copy(a, b, sems.at[1, n]) for n, (a, b) in enumerate(zip(held, results))]
+    for read in reads:
+        read.start()
+    for read, write in zip(reads, writes):
+        read.wait()
+        write.start()
+    for write in writes:
+        write.wait()
+
+
+def hand_over(arrays):
+    count = len(arrays)
+    return pl.pallas_call(
+        functools.partial(hand_over_kernel, count),
+        out_shape=[jax.ShapeDtypeStruct(a.shape, a.dtype) for a in arrays],
+        in_specs=[ANY] * count,
+        out_specs=[ANY] * count,
+        scratch_shapes=[pltpu.VMEM(a.shape, a.dtype) for a in arrays] + [DMA((2, count))],
+        compiler_params=pltpu.CompilerParams(vmem_limit_bytes=62 << 20),
+        name="hand_over",
+    )(*arrays)
 
 
 def shards(
@@ -1138,7 +1158,9 @@
     results = backward(shape, with_slab, tokens, cotangent, *kept)
     output, grad_tokens, gate_grad, up_grad, down_grad = results[:5]
     if with_slab:
-        out_grad, query_grad, keyval_grad, gain_grad = results[5:]
+        *arrays, gain_grad = results
+        output, grad_tokens, gate_grad, up_grad, down_grad, out_grad, query_grad, keyval_grad = hand_over(
+            arrays)
     else:
         out_grad, query_grad, rest_grad = [
             lax.psum_scatter(g.astype(F32), ("row", "col"), scatter_dimension=0, tiled=True)

time: 229 us -> 222 us (0.969)
  local copies, waits for them, and re-layouts: 10.1 us -> 1.41 us
    unnamed x22 -> x2, local copies, waits for them, and re-layouts: 7.77 us -> 0.01 us
    pallas_call x0 -> x1, Pallas kernels: none -> 3.84 us  [hand_over(): pl.pallas_call(functools.partial(hand_over_kernel, count), out_shape=[jax...]
    pallas_call x1, Pallas kernels: 93.4 us -> 90.5 us  [backward(): pl.pallas_call(functools.partial(backward_kernel, shape, with_slab, (D, T...]
where the time goes in v3:
time: 222 us; the launch traced here: 221 us
  Pallas kernels  219 us (99%)
    pallas_call x1, Pallas kernels, forward(): pl.pallas_call(functools.partial(forward_kernel, shape, with_slab, (D, T,...  124 us
    pallas_call x1, Pallas kernels, backward(): pl.pallas_call(functools.partial(backward_kernel, shape, with_slab, (D, T...  90.5 us

profile of v3, /device:TPU:0, one launch (start us, length us, event | category | flops | bytes accessed | tf_op | source)
XLA Modules:
  0.0 221.4 jit_solution(15665788118552438595)
XLA Ops:
  0.6 0.7 pad_maximum_fusion
  1.3 0.1 copy.25
  1.4 0.6 pad.4.refs_8_
  2.0 124.3 %forward.1 = (f32[512,1024]{1,0:T(8,128)}, f32[512,1024]{1,0:T(8,128)}, f32[512,1024]{1,0:T(8,128)}, bf16[512,1024]{1,0:T(8,128)(2,1)}, f32[8,1024]{1,0:T(8,128)...) custom-call(bf16[512,1024]{1,0:T(8,128)(2,1)} %refs_0_.3, ...), custom_call_target="tpu_custom_call" | custom-call | tf_op jit(solution)/shard_map/forward/pallas_call | solution.py:731
  126.3 90.5 %backward.1 = (bf16[512,1024]{1,0:T(8,128)(2,1)}, f32[512,1024]{1,0:T(8,128)}, f32[256,384]{1,0:T(8,128)}, f32[256,384]{1,0:T(8,128)}, f32[384,256]{1,0:T(8,128)...) custom-call(bf16[512,1024]{1,0:T(8,128)(2,1)} %refs_0_.3, ...), custom_call_target="tpu_custom_call" | custom-call | tf_op jit(solution)/shard_map/backward/pallas_call | solution.py:1109
  216.8 0.0 copy-start
  216.8 3.8 %hand_over.1 = (bf16[512,1024]{1,0:T(8,128)(2,1)}, f32[512,1024]{1,0:T(8,128)}, f32[256,384]{1,0:T(8,128)}, f32[256,384]{1,0:T(8,128)}, f32[384,256]{1,0:T(8,128...) custom-call(bf16[512,1024]{1,0:T(8,128)(2,1)} %get-tuple-element.51.refs_0_, ...), custom_call_target="tpu_custom_call" | custom-call | tf_op jit(solution)/shard_map/hand_over/pallas_call | solution.py:1137
  220.7 0.0 copy-done
  220.7 0.7 slice_reduce_fusion
Async XLA Ops:
  216.8 3.9 %copy-start = (f32[32,128]{1,0:T(8,128)S(1)}, f32[32,128]{1,0:T(8,128)}, u32[]{:S(2)}) copy-start(f32[32,128]{1,0:T(8,128)} %get-tuple-element.61) | copy-start | bytes 49156

commit v4 on v3

--- a/solution.py
+++ b/solution.py
@@ -1000,6 +1000,9 @@
 
     window[pl.ds(0, T)] = kv_grad[...].astype(BF)
 
+    for s in order[:-1]:
+        far.third(s)
+
     def keyval_weight_grad(t):
         put(weight_grads[2], t, slice(0, 2 * DH), product(attn_in_t[at(t, BLOCK)], window[pl.ds(0, T)]))
 
@@ -1026,8 +1029,6 @@
     loop(D // BLOCK, gain_grad)
     if with_slab:
         near_rest = Near(2)
-    for s in order[:-1]:
-        far.third(s)
     if with_slab:
         near_query.second()
         near_rest.fold()

time: 222 us -> 218 us (0.982)
  Pallas kernels: 219 us -> 216 us
    pallas_call x1, Pallas kernels: 90.5 us -> 87.4 us  [backward(): pl.pallas_call(functools.partial(backward_kernel, shape, with_slab, (D, T...]
where the time goes in v4:
time: 218 us
  Pallas kernels  216 us (99%)
    pallas_call x1, Pallas kernels, forward(): pl.pallas_call(functools.partial(forward_kernel, shape, with_slab, (D, T,...  124 us
    pallas_call x1, Pallas kernels, backward(): pl.pallas_call(functools.partial(backward_kernel, shape, with_slab, (D, T...  87.4 us

profile of v4, /device:TPU:0, one launch (start us, length us, event | category | flops | bytes accessed | tf_op | source)
XLA Modules:
  0.0 218.3 jit_solution(10500304862953110137)
XLA Ops:
  0.6 0.7 pad_maximum_fusion
  1.3 0.1 copy.25
  1.4 0.6 pad.4.refs_8_
  2.0 124.3 %forward.1 = (f32[512,1024]{1,0:T(8,128)}, f32[512,1024]{1,0:T(8,128)}, f32[512,1024]{1,0:T(8,128)}, bf16[512,1024]{1,0:T(8,128)(2,1)}, f32[8,1024]{1,0:T(8,128)...) custom-call(bf16[512,1024]{1,0:T(8,128)(2,1)} %refs_0_.3, ...), custom_call_target="tpu_custom_call" | custom-call | tf_op jit(solution)/shard_map/forward/pallas_call | solution.py:731
  126.3 87.4 %backward.1 = (bf16[512,1024]{1,0:T(8,128)(2,1)}, f32[512,1024]{1,0:T(8,128)}, f32[256,384]{1,0:T(8,128)}, f32[256,384]{1,0:T(8,128)}, f32[384,256]{1,0:T(8,128)...) custom-call(bf16[512,1024]{1,0:T(8,128)(2,1)} %refs_0_.3, ...), custom_call_target="tpu_custom_call" | custom-call | tf_op jit(solution)/shard_map/backward/pallas_call | solution.py:1110
  213.7 0.0 copy-start
  213.7 3.8 %hand_over.1 = (bf16[512,1024]{1,0:T(8,128)(2,1)}, f32[512,1024]{1,0:T(8,128)}, f32[256,384]{1,0:T(8,128)}, f32[256,384]{1,0:T(8,128)}, f32[384,256]{1,0:T(8,128...) custom-call(bf16[512,1024]{1,0:T(8,128)(2,1)} %get-tuple-element.51.refs_0_, ...), custom_call_target="tpu_custom_call" | custom-call | tf_op jit(solution)/shard_map/hand_over/pallas_call | solution.py:1138
  217.6 0.0 copy-done
  217.6 0.7 slice_reduce_fusion
Async XLA Ops:
  213.7 3.9 %copy-start = (f32[32,128]{1,0:T(8,128)S(1)}, f32[32,128]{1,0:T(8,128)}, u32[]{:S(2)}) copy-start(f32[32,128]{1,0:T(8,128)} %get-tuple-element.61) | copy-start | bytes 49156
